TPU v7x, 256 devices: a whole 4x4x8 slice. The times are simulated.
256 devices in a mesh: sample: 4 (over y_lo, core), row: 16 (over z, y_hi), col: 4 (over x).
Axes of the slice: x: 4, y: 4 (y_hi: 2, y_lo: 2; y = y_hi * 2 + y_lo), z: 8, core: 2. Of those that a mesh axis runs over, the one named last changes fastest.
Arguments:
- trunk_pair: bfloat16 [1024, 1024, 128], P('row', 'col'), may hold values from -6 to 6
- distance_bins: int32 [4, 1024, 1024], P('sample', 'row', 'col'), may hold values from 0 to 38
- token_mask: int32 [1024], replicated, may hold values 0 or 1
- single: bfloat16 [1024, 384], P('row', 'sample'), may hold values from -6 to 6
- dist_weight: bfloat16 [39, 128], replicated, may hold values from -5 to 5
- pair_gain: float32 [128], replicated, may hold values from 0.1 to 1.9
- bias_weight: bfloat16 [128, 16], replicated
- single_gain: float32 [384], replicated, may hold values from 0.1 to 1.9
- query_weight: bfloat16 [384, 384], P(None, 'col'), may hold values from -0.3125 to 0.3125
- query_bias: float32 [384], P('col'), may hold values from -3 to 3
- key_weight: bfloat16 [384, 384], P(None, 'col'), may hold values from -0.3125 to 0.3125
- value_weight: bfloat16 [384, 384], P(None, 'col'), may hold values from -0.3125 to 0.3125
- gate_weight: bfloat16 [384, 384], P(None, 'col'), may hold values from -0.3125 to 0.3125
- out_weight: bfloat16 [384, 384], P('col'), may hold values from -0.3125 to 0.3125
Outputs:
- single_update: bfloat16 [4, 1024, 384], P('sample', 'row', 'col')
All inputs are finite; a program needn't handle non-finite values.
Results may differ from a plain program's by a relative error of at most 0.015.
The roundings to bfloat16 on the way count: a program that leaves them out, or rounds other values in their place, can miss the bound.
Values may be sent and summed in bfloat16 or wider, within the bound.
No kernel may reach another device: no remote copies, remote signals or barrier semaphores. Data moves between devices by JAX's collectives and lax.ppermute only.
A program may use at most 64 MiB of HBM per device.

v0:
```python
import jax
import jax.numpy as jnp
from jax import lax
from jax.sharding import PartitionSpec as P


def layer_norm(values, gain):
    mean = jnp.mean(values, axis=-1, keepdims=True)
    centered = values - mean
    var = jnp.mean(centered * centered, axis=-1, keepdims=True)
    return centered * lax.rsqrt(var + 1e-05) * gain


def attend_block(carry, q_heads, key_block, value_block, bias_part, mask_part):
    running_max, running_sum, running_acc = carry
    scale = 1.0 / jnp.sqrt(jnp.float32(q_heads.shape[2]))
    scores = (
        jnp.einsum("hqd,khd->hqk", q_heads, key_block, preferred_element_type=jnp.float32) * scale
    )
    scores = scores + bias_part.astype(jnp.float32)
    scores = scores + ((mask_part.astype(jnp.float32) - 1.0) * 1000000000.0)[None, None, :]
    new_max = jnp.maximum(running_max, jnp.max(scores, axis=-1))
    weights = jnp.exp(scores - new_max[..., None])
    new_sum = jnp.sum(weights, axis=-1)
    contrib = jnp.einsum(
        "hqk,khd->hqd",
        weights.astype(jnp.bfloat16),
        value_block,
        preferred_element_type=jnp.float32,
    )
    return (new_max, new_sum, contrib)


def body(
    trunk_pair,
    distance_bins,
    token_mask,
    single,
    dist_weight,
    pair_gain,
    bias_weight,
    single_gain,
    query_weight,
    query_bias,
    key_weight,
    value_weight,
    gate_weight,
    out_weight,
):
    heads_total = bias_weight.shape[1]
    channels = trunk_pair.shape[2]
    group_width = query_weight.shape[1]
    head_dim = single_gain.shape[0] // heads_total
    group_heads = group_width // head_dim
    tile_rows = trunk_pair.shape[0]
    tile_cols = trunk_pair.shape[1]
    whole_single = lax.all_gather(single, "sample", axis=1, tiled=True)
    single_normed = layer_norm(whole_single.astype(jnp.float32), single_gain).astype(jnp.bfloat16)
    queries = (
        jnp.dot(single_normed, query_weight, preferred_element_type=jnp.float32) + query_bias
    ).astype(jnp.bfloat16)
    gate = jax.nn.sigmoid(jnp.dot(single_normed, gate_weight, preferred_element_type=jnp.float32))
    key_value_weight = jnp.concatenate([key_weight, value_weight], axis=1)
    padded_table = jnp.concatenate(
        [dist_weight, jnp.zeros((128 - dist_weight.shape[0], channels), jnp.bfloat16)], axis=0
    )
    onehot = (distance_bins[0][..., None] == jnp.arange(128, dtype=jnp.int32)).astype(jnp.bfloat16)
    embedded = jnp.dot(onehot.reshape(-1, 128), padded_table, preferred_element_type=jnp.float32)
    pair_s = trunk_pair.reshape(-1, channels).astype(jnp.float32) + embedded
    pair_normed = layer_norm(pair_s, pair_gain).astype(jnp.bfloat16)
    bias_tile = lax.dot_general(
        bias_weight, pair_normed, (((0,), (1,)), ((), ())), preferred_element_type=jnp.float32
    )
    bias_tile = bias_tile.astype(jnp.bfloat16).reshape(heads_total, tile_rows, tile_cols)
    q_heads = jnp.transpose(queries.reshape(tile_rows, group_heads, head_dim), (1, 0, 2))
    bias_heads = lax.all_to_all(bias_tile, "col", split_axis=0, concat_axis=2, tiled=True)
    start_carry = (
        jnp.full((group_heads, tile_rows), -1e30, jnp.float32),
        jnp.zeros((group_heads, tile_rows), jnp.float32),
        jnp.zeros((group_heads, tile_rows, head_dim), jnp.float32),
    )
    piece = lax.all_gather(single_normed, "row", axis=0, tiled=True)
    count = piece.shape[0]
    projected = jnp.dot(piece, key_value_weight, preferred_element_type=jnp.float32).astype(
        jnp.bfloat16
    )
    key_block = projected[:, :group_width].reshape(count, group_heads, head_dim)
    value_block = projected[:, group_width:].reshape(count, group_heads, head_dim)
    final_max, final_sum, final_acc = attend_block(
        start_carry, q_heads, key_block, value_block, bias_heads, token_mask
    )
    attended = final_acc / final_sum[..., None]
    attended = jnp.transpose(attended, (1, 0, 2)).reshape(tile_rows, group_width)
    gated = (gate * attended).astype(jnp.bfloat16)
    partial_update = jnp.dot(gated, out_weight, preferred_element_type=jnp.float32)
    update = lax.psum_scatter(partial_update, "col", scatter_dimension=1, tiled=True)
    return update.astype(jnp.bfloat16)[None]


def solution(mesh):
    placed = (
        P("row", "col", None),
        P("sample", "row", "col"),
        P(),
        P("row", "sample"),
        P(),
        P(),
        P(),
        P(),
        P(None, "col"),
        P("col"),
        P(None, "col"),
        P(None, "col"),
        P(None, "col"),
        P("col", None),
    )
    return jax.shard_map(
        body, mesh=mesh, in_specs=placed, out_specs=P("sample", "row", "col"), check_vma=False
    )
```

profile of v0, /device:TPU:8, one launch (start us, length us, event | category | flops | bytes accessed | tf_op | source)
XLA Modules:
  0.0 121.4 jit_solution(10705247466023171844)
XLA Ops:
  6.5 5.1 %bitcast_convert_fusion = f32[16384,128]{1,0:T(8,128)} fusion(bf16[64,256,128]{2,1,0:T(8,128)(2,1)} %param.14), kind=kLoop, calls=%fused_computation.5 | loop fusion | flops 2097152 | bytes 12582912 | tf_op jit(solution)/shard_map/convert_element_type | solution.py:69
  11.7 9.1 %copy.31 = f32[16384,128]{0,1:T(8,128)} copy(f32[16384,128]{1,0:T(8,128)} %bitcast_convert_fusion) | data formatting | bytes 16777216 | tf_op jit(solution)/shard_map/convert_element_type | solution.py:69
  20.8 7.9 %fusion.26 = (f32[16384]{0:T(1024)S(1)}, f32[16384,128]{0,1:T(8,128)S(1)}) fusion(f32[16384,128]{0,1:T(8,128)} %copy.31, bf16[39,128]{1,0:T(8,128)(2,1)S(1)} %copy-done.7, s32[16384]{0:T(1024)S(1)} %bitcast.53), kind=kOutput, calls=%fused_computation.49 | convolution fusion | flops 543145984 | bytes 16918272 | tf_op jit(solution)/shard_map/dot_general | solution.py:68
  28.8 1.0 multiply_reduce_fusion
  29.9 1.1 convolution_convert_fusion
  31.0 0.9 copy.36
  31.9 4.3 %all-to-all-start = ((bf16[16,64,256]{2,1,0:T(8,128)(2,1)}), bf16[16,64,256]{2,1,0:T(8,128)(2,1)S(1)}, u32[]{:S(2)}, u32[]{:S(2)}) async-start(bf16[16,64,256]{2,1,0:T(8,128)(2,1)} %bitcast.27), calls=%async_computation | async-start | bytes 1048576 | tf_op jit(solution)/shard_map/all_to_all | solution.py:76
  36.2 5.2 %all-gather = bf16[4,96,64]{1,2,0:T(8,128)(2,1)S(1)} all-gather(bf16[1,96,64]{1,2,0:T(8,128)(2,1)S(1)} %bitcast.58), channel_id=1, replica_groups=mesh['sample'=4,'row'=16,'col'=4] {'sample'}, dimensions={0}, use_global_device_ids=true | all-gather | bytes 61440 | tf_op jit(solution)/shard_map/all_gather | solution.py:57
  41.5 0.1 convert_reduce_fusion
  41.6 0.1 reshape.68
  41.8 0.2 multiply_reduce_fusion.1
  42.0 0.1 bitcast_convert_fusion.1
  42.0 47.7 %all_gather.7 = bf16[1024,384]{1,0:T(8,128)(2,1)S(1)} all-gather(bf16[64,384]{1,0:T(8,128)(2,1)S(1)} %bitcast_convert_fusion.1), channel_id=1, replica_groups=mesh['sample'=4,'row'=16,'col'=4] {'row'}, dimensions={0}, use_global_device_ids=true | all-gather | bytes 835584 | tf_op jit(solution)/shard_map/all_gather | solution.py:82
  89.8 0.2 fusion.12
  90.0 0.1 copy.27
  90.1 0.4 convolution_convert_fusion.1
  90.6 0.1 convert_bitcast_fusion
  90.7 0.1 copy.34
  90.8 0.4 fusion.27
  91.3 0.3 fusion.13
  91.6 0.3 fusion.6
  92.1 1.0 convolution_bitcast_fusion
  93.1 19.9 %reduce-scatter.4.cloned.1.call-done = f32[96,64]{1,0:T(8,128)} async-done(((f32[384,64]{1,0:T(8,128)}), f32[96,64]{1,0:T(8,128)}) %reduce-scatter.4.cloned.1.call-update) | async-done | bytes 24592
  113.0 1.5 %copy.33 = bf16[64,96]{1,0:T(8,128)(2,1)} copy(f32[64,96]{0,1:T(8,128)} %bitcast.57) | data formatting | bytes 36864
  (39 shorter events, 0.3 us)
Async XLA Ops:
  6.5 85.5 %copy-start = (bf16[96,384]{1,0:T(8,128)(2,1)S(1)}, bf16[96,384]{1,0:T(8,128)(2,1)}, u32[]{:S(2)}) copy-start(bf16[96,384]{1,0:T(8,128)(2,1)} %param.27) | copy-start | bytes 221188
  11.7 9.1 %copy-start.5 = (s32[1,64,256]{2,1,0:T(8,128)S(1)}, s32[1,64,256]{2,1,0:T(8,128)}, u32[]{:S(2)}) copy-start(s32[1,64,256]{2,1,0:T(8,128)} %param.15) | copy-start | bytes 196612
  11.7 9.1 %copy-start.7 = (bf16[39,128]{1,0:T(8,128)(2,1)S(1)}, bf16[39,128]{1,0:T(8,128)(2,1)}, u32[]{:S(2)}) copy-start(bf16[39,128]{1,0:T(8,128)(2,1)} %param.18) | copy-start | bytes 29956
  28.7 1.1 copy-start.8
  28.7 1.1 copy-start.11
  28.8 7.4 %copy-start.6 = (bf16[64,96]{1,0:T(8,128)(2,1)S(1)}, bf16[64,96]{1,0:T(8,128)(2,1)}, u32[]{:S(2)}) copy-start(bf16[64,96]{1,0:T(8,128)(2,1)} %param.17) | copy-start | bytes 36868
  28.8 13.2 %copy-start.10 = (f32[384]{0:T(512)S(1)}, f32[384]{0:T(512)}, u32[]{:S(2)}) copy-start(f32[384]{0:T(512)} %param.21) | copy-start | bytes 4612
  29.8 60.0 %copy-start.1 = (bf16[384,96]{0,1:T(8,128)(2,1)S(1)}, bf16[384,96]{0,1:T(8,128)(2,1)}, u32[]{:S(2)}) copy-start(bf16[384,96]{0,1:T(8,128)(2,1)} %param.22) | copy-start | bytes 221188
  29.8 60.0 %copy-start.12 = (f32[96]{0:T(128)S(1)}, f32[96]{0:T(128)}, u32[]{:S(2)}) copy-start(f32[96]{0:T(128)} %param.23) | copy-start | bytes 1156
  29.8 60.3 %copy-start.3 = (bf16[384,96]{0,1:T(8,128)(2,1)S(1)}, bf16[384,96]{0,1:T(8,128)(2,1)}, u32[]{:S(2)}) copy-start(bf16[384,96]{0,1:T(8,128)(2,1)} %param.25) | copy-start | bytes 221188
  29.8 60.3 %copy-start.4 = (bf16[384,96]{0,1:T(8,128)(2,1)S(1)}, bf16[384,96]{0,1:T(8,128)(2,1)}, u32[]{:S(2)}) copy-start(bf16[384,96]{0,1:T(8,128)(2,1)} %param.24) | copy-start | bytes 221188
  29.8 60.7 %copy-start.9 = (s32[1024]{0:T(1024)S(1)}, s32[1024]{0:T(1024)}, u32[]{:S(2)}) copy-start(s32[1024]{0:T(1024)} %param.16) | copy-start | bytes 12292
  31.0 61.1 %copy-start.2 = (bf16[384,96]{0,1:T(8,128)(2,1)S(1)}, bf16[384,96]{0,1:T(8,128)(2,1)}, u32[]{:S(2)}) copy-start(bf16[384,96]{0,1:T(8,128)(2,1)} %param.26) | copy-start | bytes 221188
  31.9 58.7 %all-to-all-start = ((bf16[16,64,256]{2,1,0:T(8,128)(2,1)}), bf16[16,64,256]{2,1,0:T(8,128)(2,1)S(1)}, u32[]{:S(2)}, u32[]{:S(2)}) async-start(bf16[16,64,256]{2,1,0:T(8,128)(2,1)} %bitcast.27), calls=%async_computation | async-start | bytes 1048576 | tf_op jit(solution)/shard_map/all_to_all | solution.py:76
  36.2 76.8 %reduce-scatter.4.cloned.1.call-start = ((), (), s32[]{:S(2)}) async-start(), calls=%async_computation.2 | async-start | bytes 245760
Sparse Core Ops, SparseCore 0:
  93.2 19.7 reduce-scatter.3
where the time goes:
time: 122 us; the launch traced here: 121 us
  blocking collectives  53 us (43%)
  waiting for transfers between devices  19.9 us (16%)
  between operations  13.7 us (11%)
  local copies, waits for them, and re-layouts  12.1 us (10%)
  matrix products  11.5 us (9%)
  other arithmetic  6.93 us (6%)
  starting transfers between devices  4.29 us (4%)
    all_gather x1, blocking collectives, body(): piece = lax.all_gather(single_normed, 'row', axis=0, tiled=True)  47.7 us
    unnamed x2, waiting for transfers between devices  19.9 us
    convert_element_type x1, local copies, waits for them, and re-layouts, body(): pair_s = trunk_pair.reshape(-1, channels).astype(jnp.float32) + embedded  9.08 us
    dot_general x1, matrix products, body(): jnp.dot(onehot.reshape(-1, 128), padded_table, preferred_element_type=jnp...  7.93 us
    all_gather x1, blocking collectives, body(): whole_single = lax.all_gather(single, 'sample', axis=1, tiled=True)  5.24 us
    convert_element_type x1, other arithmetic, body(): pair_s = trunk_pair.reshape(-1, channels).astype(jnp.float32) + embedded  5.11 us
    all_to_all x1, starting transfers between devices, body(): lax.all_to_all(bias_tile, 'col', split_axis=0, concat_axis=2, tiled=True)  4.29 us
    unnamed x29, local copies, waits for them, and re-layouts  2.51 us
  transfers between devices with their start and end apart: 2, of which 1 were waited for; matrix products, arithmetic and copies ran while one was open for 1% of the time, Pallas kernels for 0%

commit v1 on v0

v1 whole, which is shorter than its diff:
```python
import functools

import jax
import jax.numpy as jnp
from jax import lax
from jax.experimental import pallas as pl
from jax.experimental.pallas import tpu as pltpu
from jax.sharding import PartitionSpec as P

F32 = jnp.float32
BF16 = jnp.bfloat16
NT = (((1,), (1,)), ((), ()))
EPS = 1e-05
VMEM = pl.BlockSpec(memory_space=pltpu.VMEM)
SMEM = pl.BlockSpec(memory_space=pltpu.SMEM)
AXES = ("sample", "row", "col")


def mm(a, b):
    return jnp.dot(a, b, preferred_element_type=F32)


def mm_nt(a, b):
    return lax.dot_general(a, b, NT, preferred_element_type=F32)


def iota(shape, dim):
    return lax.broadcasted_iota(jnp.int32, shape, dim)


def pair_kernel(
    pair_ref, bins_ref, table_ref, gain_ref, weight_ref, bias_ref, centre, table_t, gain_b
):
    rows, cols, chans = pair_ref.shape
    bins_count = table_ref.shape[0]

    @pl.when(pl.program_id(0) == 0)
    def _():
        eye = (iota((chans, chans), 0) == iota((chans, chans), 1)).astype(F32)
        centre[...] = (eye - 1.0 / chans).astype(BF16)
        table = table_ref[...].astype(F32)
        table = table - jnp.mean(table, axis=1, keepdims=True)
        high = table.astype(BF16).astype(F32)
        low = (table - high).astype(BF16).astype(F32)
        gap = jnp.zeros((48 - bins_count, chans), F32)
        tail = jnp.zeros((chans - 96, chans), F32)
        stacked = jnp.concatenate([high, gap, low, gap, tail], axis=0)
        table_t[...] = jnp.transpose(stacked)[:, :96].astype(BF16)
        gain_rows = jnp.broadcast_to(gain_ref[...], (chans, chans))
        gain_t = jnp.transpose(gain_rows)
        gain_b[...] = jnp.concatenate([gain_t] * (cols // chans), axis=1)

    weight = weight_ref[...]
    for i in range(rows):
        bins = bins_ref[pl.ds(i, 1), :]
        onehot = (iota((48, cols), 0) == bins).astype(F32).astype(BF16)
        onehot = jnp.concatenate([onehot, onehot], axis=0)
        centred = mm_nt(centre[...], pair_ref[i]) + mm(table_t[...], onehot)
        var = jnp.mean(centred * centred, axis=0, keepdims=True)
        scaled = (centred * gain_b[...]).astype(BF16)
        bias = mm(weight, scaled) * lax.rsqrt(var + EPS)
        bias_ref[i] = bias.astype(BF16)


def pair_bias(pair, bins, table, gain, weight_t, start, count, step):
    chans = pair.shape[2]
    cols = pair.shape[1]
    heads = weight_t.shape[0]
    first = start // step
    return pl.pallas_call(
        pair_kernel,
        grid=(count // step,),
        in_specs=[
            pl.BlockSpec((step, cols, chans), lambda i: (first + i, 0, 0)),
            pl.BlockSpec((step, cols), lambda i: (first + i, 0)),
            pl.BlockSpec(table.shape, lambda i: (0, 0)),
            pl.BlockSpec(gain.shape, lambda i: (0, 0)),
            pl.BlockSpec(weight_t.shape, lambda i: (0, 0)),
        ],
        out_specs=pl.BlockSpec((step, heads, cols), lambda i: (i, 0, 0)),
        out_shape=jax.ShapeDtypeStruct((count, heads, cols), BF16),
        scratch_shapes=[
            pltpu.VMEM((chans, chans), BF16),
            pltpu.VMEM((chans, 96), BF16),
            pltpu.VMEM((chans, cols), F32),
        ],
        compiler_params=pltpu.CompilerParams(vmem_limit_bytes=16 * 2**20),
        cost_estimate=pl.CostEstimate(
            flops=count * cols * 65536, bytes_accessed=count * cols * 300, transcendentals=0
        ),
        name="pair_bias",
    )(pair, bins, table, gain, weight_t)


def pack_kernel(ids, wq, wk, wv, wg, wo, qb, pay1_ref, pay2_ref, own_ref):
    core, col = ids[0], ids[1]
    group, width = wq.shape
    tiles = width // 128
    ws = (wq, wk, wv, wg)
    for w in range(4):
        for t in range(tiles):
            at = (w * tiles + t) * group
            pay1_ref[at : at + group, :] = ws[w][:, 128 * t : 128 * t + 128]
    base = 4 * tiles * group
    half = 2 * tiles * group

    @pl.when(core == 0)
    def _():
        pay2_ref[0:half, :] = pay1_ref[0:half, :]

    @pl.when(core != 0)
    def _():
        pay2_ref[0:half, :] = pay1_ref[half : 2 * half, :]

    shift = qb[...]
    high = shift.astype(BF16).astype(F32)
    low = shift - high
    lane = iota((group, 128), 1)

    def tail(dest):
        pick = (iota((width, 128), 0) - dest * group == iota((width, 128), 1)) & (
            iota((width, 128), 1) < group
        )
        cut = mm(wo[...], pick.astype(F32).astype(BF16))
        cut = jnp.where(lane == group, high, cut)
        cut = jnp.where(lane == group + 1, low, cut)
        return cut.astype(BF16)

    pay1_ref[base : base + group, :] = tail(lax.rem(col + 5 - 2 * core, 4))
    pay2_ref[half : half + group, :] = tail(lax.rem(col + 2, 4))
    own_ref[...] = tail(col)


def pack(ids, wq, wk, wv, wg, wo, qb):
    group, width = wq.shape
    tiles = width // 128
    return pl.pallas_call(
        pack_kernel,
        in_specs=[SMEM] + [VMEM] * 6,
        out_specs=[VMEM] * 3,
        out_shape=[
            jax.ShapeDtypeStruct(((4 * tiles + 1) * group, 128), BF16),
            jax.ShapeDtypeStruct(((2 * tiles + 1) * group, 128), BF16),
            jax.ShapeDtypeStruct((group, 128), BF16),
        ],
        compiler_params=pltpu.CompilerParams(vmem_limit_bytes=16 * 2**20),
        cost_estimate=pl.CostEstimate(flops=10**8, bytes_accessed=10**6, transcendentals=0),
        name="pack_weights",
    )(ids, wq, wk, wv, wg, wo, qb)


def attend_kernel(
    ids, mn, sib, wq, wk, wv, wg, own_t, p1, p2, s1, s2, gain, mask, bias_a, bias_b,
    msg_ref, gate_ref, wo_ref, x_all, w_all,
):
    core, col, ylo, rlow = ids[0], ids[1], ids[2], ids[3]
    group, width = wq.shape
    tiles = width // 128
    heads = bias_a.shape[1]
    head_dim = width // heads
    tok = 64
    keys = 256

    def place(dest, w, t, value):
        at = pl.multiple_of(dest * group, 32)
        w_all[w, pl.ds(at, group), 128 * t : 128 * t + 128] = value

    def place_tail(dest, value):
        wo_ref[pl.ds(pl.multiple_of(dest * group, 32), group), :] = value

    before, after, across = lax.rem(col + 3, 4), lax.rem(col + 1, 4), lax.rem(col + 2, 4)
    mine = jnp.where(core == 0, before, after)
    other = jnp.where(core == 0, after, before)
    own = (wq, wk, wv, wg)
    for w in range(4):
        w_all[w, pl.ds(pl.multiple_of(col * group, 32), group), :] = own[w][...]
        for t in range(tiles):
            at = (w * tiles + t) * group
            place(mine, w, t, p1[at : at + group, :])
            place(other, w, t, s1[at : at + group, :])
    for w in range(2):
        for t in range(tiles):
            at = (w * tiles + t) * group
            a, b = p2[at : at + group, :], s2[at : at + group, :]
            place(across, w, t, jnp.where(core == 0, a, b))
            place(across, w + 2, t, jnp.where(core == 0, b, a))
    base = 4 * tiles * group
    half = 2 * tiles * group
    place_tail(col, own_t[...])
    place_tail(mine, p1[base : base + group, :])
    place_tail(other, s1[base : base + group, :])
    place_tail(across, p2[half : half + group, :])

    span = mn.shape[0] // 2
    shard = mn.shape[1]
    for who, ref in ((0, mn), (1, sib)):
        for k in range(2):
            block = lax.rem(rlow + 2 * core + 2 * who + k, 4)
            rows = pl.ds(pl.multiple_of(block * tok, tok), tok)
            for q in range(2):
                at = 2 * tok * k + tok * q
                a = ref[at : at + tok, :].astype(F32)
                b = ref[span + at : span + at + tok, :].astype(F32)
                x_all[rows, shard * q : shard * q + shard] = jnp.where(ylo == 0, a, b)
                x_all[rows, shard * (q + 2) : shard * (q + 3)] = jnp.where(ylo == 0, b, a)
    at = 4 * tok
    quarters = (
        mn[at : at + tok, :].astype(F32),
        mn[span + at : span + at + tok, :].astype(F32),
        sib[at : at + tok, :].astype(F32),
        sib[span + at : span + at + tok, :].astype(F32),
    )
    here = [jnp.where(core == 0, quarters[0], quarters[2]), jnp.where(core == 0, quarters[2], quarters[0])]
    there = [jnp.where(core == 0, quarters[1], quarters[3]), jnp.where(core == 0, quarters[3], quarters[1])]
    for q in range(2):
        x_all[keys : keys + tok, shard * q : shard * q + shard] = jnp.where(ylo == 0, here[q], there[q])
        x_all[keys : keys + tok, shard * (q + 2) : shard * (q + 3)] = jnp.where(ylo == 0, there[q], here[q])

    x = x_all[...]
    centred = x - jnp.mean(x, axis=1, keepdims=True)
    var = jnp.mean(centred * centred, axis=1, keepdims=True)
    normed = (centred * lax.rsqrt(var + EPS) * gain[...]).astype(BF16)
    key_rows, query_rows = normed[:keys], normed[keys:]
    keys_all = mm_nt(key_rows, w_all[1]).astype(BF16)
    values_all = mm_nt(key_rows, w_all[2]).astype(BF16)
    lanes = iota((tok, 128), 1)
    ones = ((lanes == group) | (lanes == group + 1)).astype(F32).astype(BF16)
    queries = (mm_nt(query_rows, w_all[0]) + mm_nt(ones, wo_ref[...])).astype(BF16)
    gate_ref[...] = jax.nn.sigmoid(mm_nt(query_rows, w_all[3]))

    lane_w = iota((heads, width), 1)
    head_w = iota((heads, width), 0)
    head_mask = ((lane_w >= head_w * head_dim) & (lane_w < (head_w + 1) * head_dim)).astype(F32)
    key_term = (mask[pl.ds(col, 1), :].astype(F32) - 1.0) * 1000000000.0
    scale = 1.0 / jnp.sqrt(jnp.float32(head_dim))
    part = 16
    rows = part * heads
    spread = (iota((rows, part), 0) // heads == iota((rows, part), 1)).astype(F32).astype(BF16)
    gather = (iota((part, rows), 1) // heads == iota((part, rows), 0)).astype(F32).astype(BF16)
    lane_s = iota((rows, 128), 1)
    slot = lane_s // heads
    mine_lane = (lane_s % heads) == (iota((rows, 128), 0) % heads)
    for p in range(tok // part):
        ref = bias_a if p < 2 else bias_b
        at = part * (p % 2)
        bias = ref[at : at + part].astype(F32).reshape(rows, keys)
        wide = mm(spread, queries[part * p : part * p + part])
        wide = (wide.reshape(part, heads, width) * head_mask[None]).reshape(rows, width).astype(BF16)
        scores = mm_nt(wide, keys_all) * scale + bias + key_term
        top = jnp.max(scores, axis=1, keepdims=True)
        weights = jnp.exp(scores - top)
        total = jnp.sum(weights, axis=1, keepdims=True)
        out = mm(weights.astype(BF16), values_all) / total
        out = (out.reshape(part, heads, width) * head_mask[None]).reshape(rows, width).astype(BF16)
        t1 = top.astype(BF16).astype(F32)
        t2 = (top - t1).astype(BF16).astype(F32)
        t3 = top - t1 - t2
        l1 = total.astype(BF16).astype(F32)
        l2 = total - l1
        stats = jnp.where(slot == 0, t1, jnp.where(slot == 1, t2, jnp.where(slot == 2, t3, jnp.where(slot == 3, l1, l2))))
        stats = jnp.where(mine_lane & (slot < 5), stats, 0.0).astype(BF16)
        both = mm(gather, jnp.concatenate([out, stats], axis=1))
        msg_ref[part * p : part * p + part, :] = both.astype(BF16)


def attend(ids, mn, sib, wq, wk, wv, wg, own_t, p1, p2, s1, s2, gain, mask, bias_a, bias_b):
    group, width = wq.shape
    return pl.pallas_call(
        attend_kernel,
        in_specs=[SMEM] + [VMEM] * 15,
        out_specs=[VMEM] * 3,
        out_shape=[
            jax.ShapeDtypeStruct((64, width + 128), BF16),
            jax.ShapeDtypeStruct((64, width), F32),
            jax.ShapeDtypeStruct((width, 128), BF16),
        ],
        scratch_shapes=[
            pltpu.VMEM((320, width), F32),
            pltpu.VMEM((4, width, width), BF16),
        ],
        compiler_params=pltpu.CompilerParams(vmem_limit_bytes=24 * 2**20),
        cost_estimate=pl.CostEstimate(flops=10**9, bytes_accessed=4 * 10**6, transcendentals=300000),
        name="attend",
    )(ids, mn, sib, wq, wk, wv, wg, own_t, p1, p2, s1, s2, gain, mask, bias_a, bias_b)


def combine_kernel(m0, m1, m2, m3, gate, wo, out_ref):
    width = gate.shape[1]
    tok = m0.shape[0]
    heads = 16
    head_dim = width // heads
    lane = iota((128, width), 1)
    row = iota((128, width), 0)
    slot = row // heads
    head = row % heads
    same = (lane >= head * head_dim) & (lane < (head + 1) * head_dim)
    pick_top = (same & (slot < 3)).astype(F32).astype(BF16)
    pick_sum = (same & ((slot == 3) | (slot == 4))).astype(F32).astype(BF16)
    parts = [m0, m1, m2, m3]
    tops = [mm(m[:, width : width + 128], pick_top) for m in parts]
    sums = [mm(m[:, width : width + 128], pick_sum) for m in parts]
    best = jnp.maximum(jnp.maximum(tops[0], tops[1]), jnp.maximum(tops[2], tops[3]))
    numer = jnp.zeros((tok, width), F32)
    denom = jnp.zeros((tok, width), F32)
    for m, top, total in zip(parts, tops, sums):
        share = jnp.exp(top - best) * total
        denom = denom + share
        numer = numer + share * m[:, :width].astype(F32)
    gated = (gate[...] * (numer / denom)).astype(BF16)
    out = mm(gated, wo[...])
    out_ref[...] = out[:, : out_ref.shape[1]].astype(BF16)


def combine(m0, m1, m2, m3, gate, wo, group):
    return pl.pallas_call(
        combine_kernel,
        in_specs=[VMEM] * 6,
        out_specs=VMEM,
        out_shape=jax.ShapeDtypeStruct((m0.shape[0], group), BF16),
        compiler_params=pltpu.CompilerParams(vmem_limit_bytes=16 * 2**20),
        name="combine",
    )(m0, m1, m2, m3, gate, wo)


def device(s, r, c):
    return (s * 16 + r) * 4 + c


def long_pairs(k):
    pairs = []
    for s in range(4):
        for rb in range(4):
            for rl in range(4):
                for c in range(4):
                    source = device(s, 4 * c + (rl + 2 * (s % 2) + k) % 4, rb)
                    pairs.append((source, device(s, 4 * rb + rl, c)))
    return pairs


CORE_PAIRS = [(i, i ^ 1) for i in range(4)]
YLO_PAIRS = [(i, i ^ 2) for i in range(4)]


def side_pairs():
    return [(4 * s + c, 4 * s + (c + 1 - 2 * (s % 2)) % 4) for s in range(4) for c in range(4)]


def shift_pairs(k):
    return [(c, (c + k) % 4) for c in range(4)]


def body(
    trunk_pair, distance_bins, token_mask, single, dist_weight, pair_gain, bias_weight,
    single_gain, query_weight, query_bias, key_weight, value_weight, gate_weight, out_weight,
):
    sample = lax.axis_index("sample")
    row = lax.axis_index("row")
    col = lax.axis_index("col")
    core = sample % 2
    ids = jnp.stack([core, col, sample // 2, row % 4]).astype(jnp.int32)
    group = query_weight.shape[1]

    wq, wk, wv, wg = (w.T for w in (query_weight, key_weight, value_weight, gate_weight))
    pay1, pay2, own_t = pack(ids, wq, wk, wv, wg, out_weight, query_bias.reshape(group, 1))

    x1 = lax.ppermute(single, "sample", CORE_PAIRS)
    xa = jnp.concatenate(
        [jnp.where(core == 0, single, x1), jnp.where(core == 0, x1, single)], axis=0
    )
    a0 = lax.ppermute(xa, AXES, long_pairs(0))
    a1 = lax.ppermute(xa, AXES, long_pairs(1))
    p1 = lax.ppermute(pay1, ("sample", "col"), side_pairs())
    p2 = lax.ppermute(pay2, "col", shift_pairs(2))

    gain = pair_gain.reshape(1, -1)
    weight_t = bias_weight.T
    bins = distance_bins[0]
    bias_a = pair_bias(trunk_pair, bins, dist_weight, gain, weight_t, 0, 32, 8)

    mine = jnp.concatenate([a0, a1, single], axis=0)
    theirs = lax.ppermute(mine, "sample", YLO_PAIRS)
    bias_b = pair_bias(trunk_pair, bins, dist_weight, gain, weight_t, 32, 32, 8)
    mn = jnp.concatenate([mine, theirs], axis=0)
    sib = lax.ppermute(mn, "sample", CORE_PAIRS)
    s1 = lax.ppermute(p1, "sample", CORE_PAIRS)
    s2 = lax.ppermute(p2, "sample", CORE_PAIRS)

    msg, gate, wo = attend(
        ids, mn, sib, wq, wk, wv, wg, own_t, p1, p2, s1, s2,
        single_gain.reshape(1, -1), token_mask.reshape(4, -1), bias_a, bias_b,
    )
    others = [lax.ppermute(msg, "col", shift_pairs(k)) for k in (1, 3, 2)]
    update = combine(msg, *others, gate, wo, group)
    return update[None]


def solution(mesh):
    placed = (
        P("row", "col", None),
        P("sample", "row", "col"),
        P(),
        P("row", "sample"),
        P(),
        P(),
        P(),
        P(),
        P(None, "col"),
        P("col"),
        P(None, "col"),
        P(None, "col"),
        P(None, "col"),
        P("col", None),
    )
    return jax.shard_map(
        body, mesh=mesh, in_specs=placed, out_specs=P("sample", "row", "col"), check_vma=False
    )
```

time: 122 us -> 69.8 us (0.57)
  blocking collectives: 53 us -> 0 us
  Pallas kernels: 0 us -> 20 us
  starting transfers between devices: 4.29 us -> 22.3 us
  between operations: 13.7 us -> 0.11 us
  matrix products: 11.5 us -> 0 us
  waiting for transfers between devices: 19.9 us -> 12.1 us
  other arithmetic: 6.93 us -> 1.55 us
    all_gather x2 -> x0, blocking collectives: 53 us -> none  [the longest x1 47.7 us: body(): piece = lax.all_gather(single_normed, 'row', axis=0, tiled=True)]
    ppermute x0 -> x12, starting transfers between devices: none -> 22.3 us  [the longest x1 11.2 us: body(): p2 = lax.ppermute(pay2, 'col', shift_pairs(2))]
    pallas_call x0 -> x5, Pallas kernels: none -> 20 us  [the longest x2 14 us: pair_bias(): pl.pallas_call(pair_kernel, grid=(count // step,), in_specs=[pl.BlockSpec...]
    unnamed x2 -> x0, waiting for transfers between devices: 19.9 us -> none
    ppermute x0 -> x12, waiting for transfers between devices: none -> 12.1 us  [the longest x1 6 us: body(): p1 = lax.ppermute(pay1, ('sample', 'col'), side_pairs())]
    dot_general x6 -> x0, matrix products: 10.4 us -> none  [the longest x1 7.93 us: body(): jnp.dot(onehot.reshape(-1, 128), padded_table, preferred_element_type=jnp...]
    convert_element_type x5 -> x0, local copies, waits for them, and re-layouts: 9.5 us -> none  [the longest x1 9.08 us: body(): pair_s = trunk_pair.reshape(-1, channels).astype(jnp.float32) + embedded]
    unnamed x29 -> x31, local copies, waits for them, and re-layouts: 2.51 us -> 10.2 us
  transfers between devices with their start and end apart: 2 -> 12, of which waited for: 1 -> 5; matrix products, arithmetic and copies ran while one was open for 1% -> 5% of each run, Pallas kernels for 0% -> 22%
where the time goes in v1:
time: 69.8 us; the launch traced here: 68.4 us
  starting transfers between devices  22.3 us (32%)
  Pallas kernels  20 us (29%)
  local copies, waits for them, and re-layouts  12.4 us (18%)
  waiting for transfers between devices  12.1 us (17%)
  other arithmetic  1.55 us (2%)
    pallas_call x2, Pallas kernels, pair_bias(): pl.pallas_call(pair_kernel, grid=(count // step,), in_specs=[pl.BlockSpec...  14 us
    ppermute x1, starting transfers between devices, body(): p2 = lax.ppermute(pay2, 'col', shift_pairs(2))  11.2 us
    unnamed x31, local copies, waits for them, and re-layouts  10.2 us
    ppermute x1, waiting for transfers between devices, body(): p1 = lax.ppermute(pay1, ('sample', 'col'), side_pairs())  6 us
    ppermute x3, waiting for transfers between devices, body(): others = [lax.ppermute(msg, 'col', shift_pairs(k)) for k in (1, 3, 2)]  4.71 us
    ppermute x3, starting transfers between devices, body(): others = [lax.ppermute(msg, 'col', shift_pairs(k)) for k in (1, 3, 2)]  4.6 us
    pallas_call x1, Pallas kernels, attend(): pl.pallas_call(attend_kernel, in_specs=[SMEM] + [VMEM] * 15, out_specs=[V...  4.06 us
    ppermute x1, starting transfers between devices, body(): a1 = lax.ppermute(xa, AXES, long_pairs(1))  3.73 us
  transfers between devices with their start and end apart: 12, of which 5 were waited for; matrix products, arithmetic and copies ran while one was open for 5% of the time, Pallas kernels for 22%

profile of v1, /device:TPU:8, one launch (start us, length us, event | category | flops | bytes accessed | tf_op | source)
XLA Modules:
  0.0 68.4 jit_solution(11150643975707475817)
XLA Ops:
  0.0 1.4 %collective-permute-done = bf16[64,96]{1,0:T(8,128)(2,1)S(1)} collective-permute-done((bf16[64,96]{1,0:T(8,128)(2,1)}, bf16[64,96]{1,0:T(8,128)(2,1)S(1)}, u32[]{:S(2)}, u32[]{:S(2)}) %collective-permute-start) | collective-permute-done | bytes 12320 | tf_op jit(solution)/shard_map/ppermute | solution.py:366
  2.1 3.7 %collective-permute-start.2 = (bf16[128,96]{1,0:T(8,128)(2,1)S(1)}, bf16[128,96]{1,0:T(8,128)(2,1)S(1)}, u32[]{:S(2)}, u32[]{:S(2)}) collective-permute-start(bf16[128,96]{1,0:T(8,128)(2,1)S(1)} %pad_maximum_fusion.1), channel_id=1, source_target_pairs={{4,0},{20,1},{36,2},{52,3},{8,4},{24,5},{40,6},{56,7},{12,8},{28,9... | collective-permute-start | bytes 73736 | tf_op jit(solution)/shard_map/ppermute | solution.py:371
  6.6 0.8 %copy.15.qb = f32[96,1]{1,0:T(8,128)S(1)} copy(f32[96,1]{0,1:T(1,128)} %bitcast.27) | data formatting | bytes 768 | tf_op jit(solution)/shard_map/reshape | solution.py:364
  7.4 0.9 %copy-done.2 = bf16[96,384]{1,0:T(8,128)(2,1)S(1)} copy-done((bf16[96,384]{1,0:T(8,128)(2,1)S(1)}, bf16[96,384]{1,0:T(8,128)(2,1)}, u32[]{:S(2)}) %copy-start.2) | copy-done | bytes 73752
  8.2 0.9 %copy-done.3 = bf16[384,96]{0,1:T(8,128)(2,1)S(1)} copy-done((bf16[384,96]{0,1:T(8,128)(2,1)S(1)}, bf16[384,96]{0,1:T(8,128)(2,1)}, u32[]{:S(2)}) %copy-start.3) | copy-done | bytes 73752
  9.1 0.9 %copy-done.5 = bf16[384,96]{0,1:T(8,128)(2,1)S(1)} copy-done((bf16[384,96]{0,1:T(8,128)(2,1)S(1)}, bf16[384,96]{0,1:T(8,128)(2,1)}, u32[]{:S(2)}) %copy-start.5) | copy-done | bytes 73752
  10.0 0.9 %copy-done.7 = bf16[384,96]{0,1:T(8,128)(2,1)S(1)} copy-done((bf16[384,96]{0,1:T(8,128)(2,1)S(1)}, bf16[384,96]{0,1:T(8,128)(2,1)}, u32[]{:S(2)}) %copy-start.7) | copy-done | bytes 73752
  10.9 0.9 %copy-done.9 = bf16[384,96]{0,1:T(8,128)(2,1)S(1)} copy-done((bf16[384,96]{0,1:T(8,128)(2,1)S(1)}, bf16[384,96]{0,1:T(8,128)(2,1)}, u32[]{:S(2)}) %copy-start.9) | copy-done | bytes 73752
  11.8 0.8 %pack_weights.1 = (bf16[1248,128]{1,0:T(8,128)(2,1)S(1)}, bf16[672,128]{1,0:T(8,128)(2,1)S(1)}, bf16[96,128]{1,0:T(8,128)(2,1)S(1)}) custom-call(s32[4]{0:T(128)S(1)} %pad_add_fusion.ids, bf16[96,384]{1,0:T(8,128)(2,1)S(1)} %bitcast.15, bf16[96,384]{1,0:T(8,128)(2,1)S(1)} %bitcast.17, bf16[96,384]{1,0:T(8,128)(2,1)S(1)} %bitcast.19, ...), custom_call_target="tpu_custom_call" | custom-call | flops 100000000 | bytes 1000000 | tf_op jit(solution)/shard_map/pack_weights/pallas_call | solution.py:137
  12.6 11.2 %collective-permute-start.6 = (bf16[672,128]{1,0:T(8,128)(2,1)S(1)}, bf16[672,128]{1,0:T(8,128)(2,1)S(1)}, u32[]{:S(2)}, u32[]{:S(2)}) collective-permute-start(bf16[672,128]{1,0:T(8,128)(2,1)S(1)} %get-tuple-element.13), channel_id=1, source_target_pairs={{0,2},{1,3},{2,0},{3,1},{4,6},{5,7},{6,4},{7,5},{8,10},{9,11},{10,... | collective-permute-start | bytes 516104 | tf_op jit(solution)/shard_map/ppermute | solution.py:373
  24.6 1.4 %collective-permute-start.3 = (bf16[320,96]{1,0:T(8,128)(2,1)S(1)}, bf16[320,96]{1,0:T(8,128)(2,1)S(1)}, u32[]{:S(2)}, u32[]{:S(2)}) collective-permute-start(bf16[320,96]{1,0:T(8,128)(2,1)S(1)} %pad_maximum_fusion), channel_id=1, source_target_pairs={{0,128},{64,192},{128,0},{192,64},{1,129},{65,193},{129,1},{193,65... | collective-permute-start | bytes 184328 | tf_op jit(solution)/shard_map/ppermute | solution.py:381
  26.0 6.0 %collective-permute-done.5.p1 = bf16[1248,128]{1,0:T(8,128)(2,1)S(1)} collective-permute-done((bf16[1248,128]{1,0:T(8,128)(2,1)S(1)}, bf16[1248,128]{1,0:T(8,128)(2,1)S(1)}, u32[]{:S(2)}, u32[]{:S(2)}) %collective-permute-start.5) | collective-permute-done | bytes 319520 | tf_op jit(solution)/shard_map/ppermute | solution.py:372
  34.8 2.2 %copy-done = bf16[64,256,128]{2,1,0:T(8,128)(2,1)S(1)} copy-done((bf16[64,256,128]{2,1,0:T(8,128)(2,1)S(1)}, bf16[64,256,128]{2,1,0:T(8,128)(2,1)}, u32[]{:S(2)}) %copy-start) | copy-done | bytes 4194328
  37.0 0.8 %copy-done.1 = s32[1,64,256]{2,1,0:T(8,128)S(1)} copy-done((s32[1,64,256]{2,1,0:T(8,128)S(1)}, s32[1,64,256]{2,1,0:T(8,128)}, u32[]{:S(2)}) %copy-start.1) | copy-done | bytes 65560
  39.9 7.0 %pair_bias.3.bias_b = bf16[32,16,256]{2,1,0:T(8,128)(2,1)S(1)} custom-call(bf16[64,256,128]{2,1,0:T(8,128)(2,1)S(1)} %copy-done, s32[64,256]{1,0:T(8,128)S(1)} %bitcast.13, bf16[39,128]{1,0:T(8,128)(2,1)S(1)} %copy-done.11, f32[1,128]{1,0:T(1,128)S(1)} %bitcast.25, bf16[16,128]{1,0:T(8,128)(2,1)S(1)} %bitcast.23), custom_call_target="tpu_custom_call" | custom-call | flops 536870912 | bytes 2457600 | tf_op jit(solution)/shard_map/pair_bias/pallas_call | solution.py:70
  46.9 7.0 %pair_bias.2.bias_a = bf16[32,16,256]{2,1,0:T(8,128)(2,1)S(1)} custom-call(bf16[64,256,128]{2,1,0:T(8,128)(2,1)S(1)} %copy-done, s32[64,256]{1,0:T(8,128)S(1)} %bitcast.14, bf16[39,128]{1,0:T(8,128)(2,1)S(1)} %copy-done.11, f32[1,128]{1,0:T(1,128)S(1)} %bitcast.26, bf16[16,128]{1,0:T(8,128)(2,1)S(1)} %bitcast.24), custom_call_target="tpu_custom_call" | custom-call | flops 536870912 | bytes 2457600 | tf_op jit(solution)/shard_map/pair_bias/pallas_call | solution.py:70
  53.9 4.1 %attend.1 = (bf16[64,512]{1,0:T(8,128)(2,1)S(1)}, f32[64,384]{1,0:T(8,128)S(1)}, bf16[384,128]{1,0:T(8,128)(2,1)S(1)}) custom-call(s32[4]{0:T(128)S(1)} %pad_add_fusion.ids, bf16[640,96]{1,0:T(8,128)(2,1)S(1)} %constant_dynamic-update-slice_fusion.mn, bf16[640,96]{1,0:T(8,128)(2,1)S(1)} %collective-permute-done.4.sib, bf16[96,384]{1,0:T(8,128)(2,1)S(1)} %bitcast.16, ...), custom_call_target="tpu_custom_call" | custom-call | flops 1000000000 | bytes 4000000 | tf_op jit(solution)/shard_map/attend/pallas_call | solution.py:268
  58.0 2.6 %collective-permute-start.11 = (bf16[64,512]{1,0:T(8,128)(2,1)S(1)}, bf16[64,512]{1,0:T(8,128)(2,1)S(1)}, u32[]{:S(2)}, u32[]{:S(2)}) collective-permute-start(bf16[64,512]{1,0:T(8,128)(2,1)S(1)} %get-tuple-element.14.m0), channel_id=1, source_target_pairs={{0,2},{1,3},{2,0},{3,1},{4,6},{5,7},{6,4},{7,5},{8,10},{9,11},{10,... | collective-permute-start | bytes 196616 | tf_op jit(solution)/shard_map/ppermute | solution.py:392
  60.6 1.3 %collective-permute-start.10 = (bf16[64,512]{1,0:T(8,128)(2,1)S(1)}, bf16[64,512]{1,0:T(8,128)(2,1)S(1)}, u32[]{:S(2)}, u32[]{:S(2)}) collective-permute-start(bf16[64,512]{1,0:T(8,128)(2,1)S(1)} %get-tuple-element.14.m0), channel_id=1, source_target_pairs={{0,3},{1,0},{2,1},{3,2},{4,7},{5,4},{6,5},{7,6},{8,11},{9,8},{10,9... | collective-permute-start | bytes 196616 | tf_op jit(solution)/shard_map/ppermute | solution.py:392
  61.8 0.8 %collective-permute-start.9 = (bf16[64,512]{1,0:T(8,128)(2,1)S(1)}, bf16[64,512]{1,0:T(8,128)(2,1)S(1)}, u32[]{:S(2)}, u32[]{:S(2)}) collective-permute-start(bf16[64,512]{1,0:T(8,128)(2,1)S(1)} %get-tuple-element.14.m0), channel_id=1, source_target_pairs={{0,1},{1,2},{2,3},{3,0},{4,5},{5,6},{6,7},{7,4},{8,9},{9,10},{10,1... | collective-permute-start | bytes 196616 | tf_op jit(solution)/shard_map/ppermute | solution.py:392
  62.6 1.4 %collective-permute-done.11.m3 = bf16[64,512]{1,0:T(8,128)(2,1)S(1)} collective-permute-done((bf16[64,512]{1,0:T(8,128)(2,1)S(1)}, bf16[64,512]{1,0:T(8,128)(2,1)S(1)}, u32[]{:S(2)}, u32[]{:S(2)}) %collective-permute-start.11) | collective-permute-done | bytes 65568 | tf_op jit(solution)/shard_map/ppermute | solution.py:392
  64.0 0.8 %collective-permute-done.10.m2 = bf16[64,512]{1,0:T(8,128)(2,1)S(1)} collective-permute-done((bf16[64,512]{1,0:T(8,128)(2,1)S(1)}, bf16[64,512]{1,0:T(8,128)(2,1)S(1)}, u32[]{:S(2)}, u32[]{:S(2)}) %collective-permute-start.10) | collective-permute-done | bytes 65568 | tf_op jit(solution)/shard_map/ppermute | solution.py:392
  64.8 2.5 %collective-permute-done.9.m1 = bf16[64,512]{1,0:T(8,128)(2,1)S(1)} collective-permute-done((bf16[64,512]{1,0:T(8,128)(2,1)S(1)}, bf16[64,512]{1,0:T(8,128)(2,1)S(1)}, u32[]{:S(2)}, u32[]{:S(2)}) %collective-permute-start.9) | collective-permute-done | bytes 65568 | tf_op jit(solution)/shard_map/ppermute | solution.py:392
  67.3 1.1 %combine.1 = bf16[64,96]{1,0:T(8,128)(2,1)} custom-call(bf16[64,512]{1,0:T(8,128)(2,1)S(1)} %get-tuple-element.14.m0, bf16[64,512]{1,0:T(8,128)(2,1)S(1)} %collective-permute-done.9.m1, bf16[64,512]{1,0:T(8,128)(2,1)S(1)} %collective-permute-done.10.m2, bf16[64,512]{1,0:T(8,128)(2,1)S(1)} %collective-permute-done.11.m3, ...), custom_call_target="tpu_custom_call" | custom-call | tf_op jit(solution)/shard_map/combine/pallas_call | solution.py:315
  (44 shorter events, 7.0 us)
Async XLA Ops:
  0.0 1.4 %collective-permute-start = (bf16[64,96]{1,0:T(8,128)(2,1)}, bf16[64,96]{1,0:T(8,128)(2,1)S(1)}, u32[]{:S(2)}, u32[]{:S(2)}) collective-permute-start(bf16[64,96]{1,0:T(8,128)(2,1)} %param.17), channel_id=1, source_target_pairs={{0,64},{64,0},{128,192},{192,128},{1,65},{65,1},{129,193},{193,129... | collective-permute-start | bytes 36872 | tf_op jit(solution)/shard_map/ppermute | solution.py:366
  2.1 21.7 %collective-permute-start.2 = (bf16[128,96]{1,0:T(8,128)(2,1)S(1)}, bf16[128,96]{1,0:T(8,128)(2,1)S(1)}, u32[]{:S(2)}, u32[]{:S(2)}) collective-permute-start(bf16[128,96]{1,0:T(8,128)(2,1)S(1)} %pad_maximum_fusion.1), channel_id=1, source_target_pairs={{4,0},{20,1},{36,2},{52,3},{8,4},{24,5},{40,6},{56,7},{12,8},{28,9... | collective-permute-start | bytes 73736 | tf_op jit(solution)/shard_map/ppermute | solution.py:371
  5.9 18.0 %collective-permute-start.1 = (bf16[128,96]{1,0:T(8,128)(2,1)S(1)}, bf16[128,96]{1,0:T(8,128)(2,1)S(1)}, u32[]{:S(2)}, u32[]{:S(2)}) collective-permute-start(bf16[128,96]{1,0:T(8,128)(2,1)S(1)} %pad_maximum_fusion.1), channel_id=1, source_target_pairs={{0,0},{16,1},{32,2},{48,3},{4,4},{20,5},{36,6},{52,7},{8,8},{24,9}... | collective-permute-start | bytes 73736 | tf_op jit(solution)/shard_map/ppermute | solution.py:370
  7.4 0.9 %copy-start.2 = (bf16[96,384]{1,0:T(8,128)(2,1)S(1)}, bf16[96,384]{1,0:T(8,128)(2,1)}, u32[]{:S(2)}) copy-start(bf16[96,384]{1,0:T(8,128)(2,1)} %wo.1) | copy-start | bytes 221188
  8.2 0.9 %copy-start.3 = (bf16[384,96]{0,1:T(8,128)(2,1)S(1)}, bf16[384,96]{0,1:T(8,128)(2,1)}, u32[]{:S(2)}) copy-start(bf16[384,96]{0,1:T(8,128)(2,1)} %param.22) | copy-start | bytes 221188
  9.1 0.9 %copy-start.5 = (bf16[384,96]{0,1:T(8,128)(2,1)S(1)}, bf16[384,96]{0,1:T(8,128)(2,1)}, u32[]{:S(2)}) copy-start(bf16[384,96]{0,1:T(8,128)(2,1)} %param.24) | copy-start | bytes 221188
  10.0 0.9 %copy-start.7 = (bf16[384,96]{0,1:T(8,128)(2,1)S(1)}, bf16[384,96]{0,1:T(8,128)(2,1)}, u32[]{:S(2)}) copy-start(bf16[384,96]{0,1:T(8,128)(2,1)} %param.25) | copy-start | bytes 221188
  10.9 0.9 %copy-start.9 = (bf16[384,96]{0,1:T(8,128)(2,1)S(1)}, bf16[384,96]{0,1:T(8,128)(2,1)}, u32[]{:S(2)}) copy-start(bf16[384,96]{0,1:T(8,128)(2,1)} %param.26) | copy-start | bytes 221188
  12.6 20.2 %collective-permute-start.6 = (bf16[672,128]{1,0:T(8,128)(2,1)S(1)}, bf16[672,128]{1,0:T(8,128)(2,1)S(1)}, u32[]{:S(2)}, u32[]{:S(2)}) collective-permute-start(bf16[672,128]{1,0:T(8,128)(2,1)S(1)} %get-tuple-element.13), channel_id=1, source_target_pairs={{0,2},{1,3},{2,0},{3,1},{4,6},{5,7},{6,4},{7,5},{8,10},{9,11},{10,... | collective-permute-start | bytes 516104 | tf_op jit(solution)/shard_map/ppermute | solution.py:373
  23.8 8.2 %collective-permute-start.5 = (bf16[1248,128]{1,0:T(8,128)(2,1)S(1)}, bf16[1248,128]{1,0:T(8,128)(2,1)S(1)}, u32[]{:S(2)}, u32[]{:S(2)}) collective-permute-start(bf16[1248,128]{1,0:T(8,128)(2,1)S(1)} %get-tuple-element.12), channel_id=1, source_target_pairs={{0,1},{1,2},{2,3},{3,0},{64,67},{65,64},{66,65},{67,66},{128,129},... | collective-permute-start | bytes 958472 | tf_op jit(solution)/shard_map/ppermute | solution.py:372
  24.6 8.7 %collective-permute-start.3 = (bf16[320,96]{1,0:T(8,128)(2,1)S(1)}, bf16[320,96]{1,0:T(8,128)(2,1)S(1)}, u32[]{:S(2)}, u32[]{:S(2)}) collective-permute-start(bf16[320,96]{1,0:T(8,128)(2,1)S(1)} %pad_maximum_fusion), channel_id=1, source_target_pairs={{0,128},{64,192},{128,0},{192,64},{1,129},{65,193},{129,1},{193,65... | collective-permute-start | bytes 184328 | tf_op jit(solution)/shard_map/ppermute | solution.py:381
  32.0 21.9 %collective-permute-start.7 = (bf16[1248,128]{1,0:T(8,128)(2,1)S(1)}, bf16[1248,128]{1,0:T(8,128)(2,1)S(1)}, u32[]{:S(2)}, u32[]{:S(2)}) collective-permute-start(bf16[1248,128]{1,0:T(8,128)(2,1)S(1)} %collective-permute-done.5.p1), channel_id=1, source_target_pairs={{0,64},{64,0},{128,192},{192,128},{1,65},{65,1},{129,193},{193,129... | collective-permute-start | bytes 958472 | tf_op jit(solution)/shard_map/ppermute | solution.py:385
  32.8 21.1 %collective-permute-start.8 = (bf16[672,128]{1,0:T(8,128)(2,1)S(1)}, bf16[672,128]{1,0:T(8,128)(2,1)S(1)}, u32[]{:S(2)}, u32[]{:S(2)}) collective-permute-start(bf16[672,128]{1,0:T(8,128)(2,1)S(1)} %collective-permute-done.6.p2), channel_id=1, source_target_pairs={{0,64},{64,0},{128,192},{192,128},{1,65},{65,1},{129,193},{193,129... | collective-permute-start | bytes 516104 | tf_op jit(solution)/shard_map/ppermute | solution.py:386
  33.3 20.6 %collective-permute-start.4 = (bf16[640,96]{1,0:T(8,128)(2,1)S(1)}, bf16[640,96]{1,0:T(8,128)(2,1)S(1)}, u32[]{:S(2)}, u32[]{:S(2)}) collective-permute-start(bf16[640,96]{1,0:T(8,128)(2,1)S(1)} %constant_dynamic-update-slice_fusion.mn), channel_id=1, source_target_pairs={{0,64},{64,0},{128,192},{192,128},{1,65},{65,1},{129,193},{193,129... | collective-permute-start | bytes 368648 | tf_op jit(solution)/shard_map/ppermute | solution.py:384
  34.8 2.2 %copy-start = (bf16[64,256,128]{2,1,0:T(8,128)(2,1)S(1)}, bf16[64,256,128]{2,1,0:T(8,128)(2,1)}, u32[]{:S(2)}) copy-start(bf16[64,256,128]{2,1,0:T(8,128)(2,1)} %pair_ref.3) | copy-start | bytes 12582916
  37.0 0.8 %copy-start.1 = (s32[1,64,256]{2,1,0:T(8,128)S(1)}, s32[1,64,256]{2,1,0:T(8,128)}, u32[]{:S(2)}) copy-start(s32[1,64,256]{2,1,0:T(8,128)} %param.15) | copy-start | bytes 196612
  37.8 0.7 %copy-start.11 = (bf16[39,128]{1,0:T(8,128)(2,1)S(1)}, bf16[39,128]{1,0:T(8,128)(2,1)}, u32[]{:S(2)}) copy-start(bf16[39,128]{1,0:T(8,128)(2,1)} %table_ref.3) | copy-start | bytes 29956
  39.9 14.1 %copy-start.4 = (bf16[384,96]{0,1:T(8,128)(2,1)S(1)}, bf16[384,96]{0,1:T(8,128)(2,1)}, u32[]{:S(2)}) copy-start(bf16[384,96]{0,1:T(8,128)(2,1)} %param.22) | copy-start | bytes 221188
  39.9 14.1 %copy-start.6 = (bf16[384,96]{0,1:T(8,128)(2,1)S(1)}, bf16[384,96]{0,1:T(8,128)(2,1)}, u32[]{:S(2)}) copy-start(bf16[384,96]{0,1:T(8,128)(2,1)} %param.24) | copy-start | bytes 221188
  39.9 14.1 %copy-start.8 = (bf16[384,96]{0,1:T(8,128)(2,1)S(1)}, bf16[384,96]{0,1:T(8,128)(2,1)}, u32[]{:S(2)}) copy-start(bf16[384,96]{0,1:T(8,128)(2,1)} %param.25) | copy-start | bytes 221188
  39.9 14.1 %copy-start.10 = (bf16[384,96]{0,1:T(8,128)(2,1)S(1)}, bf16[384,96]{0,1:T(8,128)(2,1)}, u32[]{:S(2)}) copy-start(bf16[384,96]{0,1:T(8,128)(2,1)} %param.26) | copy-start | bytes 221188
  58.0 6.0 %collective-permute-start.11 = (bf16[64,512]{1,0:T(8,128)(2,1)S(1)}, bf16[64,512]{1,0:T(8,128)(2,1)S(1)}, u32[]{:S(2)}, u32[]{:S(2)}) collective-permute-start(bf16[64,512]{1,0:T(8,128)(2,1)S(1)} %get-tuple-element.14.m0), channel_id=1, source_target_pairs={{0,2},{1,3},{2,0},{3,1},{4,6},{5,7},{6,4},{7,5},{8,10},{9,11},{10,... | collective-permute-start | bytes 196616 | tf_op jit(solution)/shard_map/ppermute | solution.py:392
  60.6 4.3 %collective-permute-start.10 = (bf16[64,512]{1,0:T(8,128)(2,1)S(1)}, bf16[64,512]{1,0:T(8,128)(2,1)S(1)}, u32[]{:S(2)}, u32[]{:S(2)}) collective-permute-start(bf16[64,512]{1,0:T(8,128)(2,1)S(1)} %get-tuple-element.14.m0), channel_id=1, source_target_pairs={{0,3},{1,0},{2,1},{3,2},{4,7},{5,4},{6,5},{7,6},{8,11},{9,8},{10,9... | collective-permute-start | bytes 196616 | tf_op jit(solution)/shard_map/ppermute | solution.py:392
  61.8 5.5 %collective-permute-start.9 = (bf16[64,512]{1,0:T(8,128)(2,1)S(1)}, bf16[64,512]{1,0:T(8,128)(2,1)S(1)}, u32[]{:S(2)}, u32[]{:S(2)}) collective-permute-start(bf16[64,512]{1,0:T(8,128)(2,1)S(1)} %get-tuple-element.14.m0), channel_id=1, source_target_pairs={{0,1},{1,2},{2,3},{3,0},{4,5},{5,6},{6,7},{7,4},{8,9},{9,10},{10,1... | collective-permute-start | bytes 196616 | tf_op jit(solution)/shard_map/ppermute | solution.py:392
  (2 other events, 1.3 us)

commit v2 on v1

--- a/solution.py
+++ b/solution.py
@@ -11,8 +11,10 @@
 BF16 = jnp.bfloat16
 NT = (((1,), (1,)), ((), ()))
 EPS = 1e-05
+BIG = 58 * 2**20
 VMEM = pl.BlockSpec(memory_space=pltpu.VMEM)
 SMEM = pl.BlockSpec(memory_space=pltpu.SMEM)
+HBM = pl.BlockSpec(memory_space=pltpu.HBM)
 AXES = ("sample", "row", "col")
 
 
@@ -28,135 +30,193 @@
     return lax.broadcasted_iota(jnp.int32, shape, dim)
 
 
-def pair_kernel(
-    pair_ref, bins_ref, table_ref, gain_ref, weight_ref, bias_ref, centre, table_t, gain_b
+def prepare_kernel(
+    ids, wq, wk, wv, wg, wo, qb, single_gain, token_mask, table, pair_gain, bias_weight,
+    pay1_ref, pay2_ref, own_w, own_t, centre, gain_b, weight_ref, sgain_ref, term_ref,
+    wo_v, qb_v, sg_v, mask_v, table_v, pg_v, sems,
 ):
-    rows, cols, chans = pair_ref.shape
-    bins_count = table_ref.shape[0]
-
-    @pl.when(pl.program_id(0) == 0)
-    def _():
-        eye = (iota((chans, chans), 0) == iota((chans, chans), 1)).astype(F32)
-        centre[...] = (eye - 1.0 / chans).astype(BF16)
-        table = table_ref[...].astype(F32)
-        table = table - jnp.mean(table, axis=1, keepdims=True)
-        high = table.astype(BF16).astype(F32)
-        low = (table - high).astype(BF16).astype(F32)
-        gap = jnp.zeros((48 - bins_count, chans), F32)
-        tail = jnp.zeros((chans - 96, chans), F32)
-        stacked = jnp.concatenate([high, gap, low, gap, tail], axis=0)
-        table_t[...] = jnp.transpose(stacked)[:, :96].astype(BF16)
-        gain_rows = jnp.broadcast_to(gain_ref[...], (chans, chans))
-        gain_t = jnp.transpose(gain_rows)
-        gain_b[...] = jnp.concatenate([gain_t] * (cols // chans), axis=1)
-
-    weight = weight_ref[...]
-    for i in range(rows):
-        bins = bins_ref[pl.ds(i, 1), :]
-        onehot = (iota((48, cols), 0) == bins).astype(F32).astype(BF16)
-        onehot = jnp.concatenate([onehot, onehot], axis=0)
-        centred = mm_nt(centre[...], pair_ref[i]) + mm(table_t[...], onehot)
-        var = jnp.mean(centred * centred, axis=0, keepdims=True)
-        scaled = (centred * gain_b[...]).astype(BF16)
-        bias = mm(weight, scaled) * lax.rsqrt(var + EPS)
-        bias_ref[i] = bias.astype(BF16)
-
-
-def pair_bias(pair, bins, table, gain, weight_t, start, count, step):
-    chans = pair.shape[2]
-    cols = pair.shape[1]
-    heads = weight_t.shape[0]
-    first = start // step
-    return pl.pallas_call(
-        pair_kernel,
-        grid=(count // step,),
-        in_specs=[
-            pl.BlockSpec((step, cols, chans), lambda i: (first + i, 0, 0)),
-            pl.BlockSpec((step, cols), lambda i: (first + i, 0)),
-            pl.BlockSpec(table.shape, lambda i: (0, 0)),
-            pl.BlockSpec(gain.shape, lambda i: (0, 0)),
-            pl.BlockSpec(weight_t.shape, lambda i: (0, 0)),
-        ],
-        out_specs=pl.BlockSpec((step, heads, cols), lambda i: (i, 0, 0)),
-        out_shape=jax.ShapeDtypeStruct((count, heads, cols), BF16),
-        scratch_shapes=[
-            pltpu.VMEM((chans, chans), BF16),
-            pltpu.VMEM((chans, 96), BF16),
-            pltpu.VMEM((chans, cols), F32),
-        ],
-        compiler_params=pltpu.CompilerParams(vmem_limit_bytes=16 * 2**20),
-        cost_estimate=pl.CostEstimate(
-            flops=count * cols * 65536, bytes_accessed=count * cols * 300, transcendentals=0
-        ),
-        name="pair_bias",
-    )(pair, bins, table, gain, weight_t)
-
-
-def pack_kernel(ids, wq, wk, wv, wg, wo, qb, pay1_ref, pay2_ref, own_ref):
     core, col = ids[0], ids[1]
     group, width = wq.shape
     tiles = width // 128
-    ws = (wq, wk, wv, wg)
-    for w in range(4):
-        for t in range(tiles):
-            at = (w * tiles + t) * group
-            pay1_ref[at : at + group, :] = ws[w][:, 128 * t : 128 * t + 128]
-    base = 4 * tiles * group
-    half = 2 * tiles * group
-
-    @pl.when(core == 0)
-    def _():
-        pay2_ref[0:half, :] = pay1_ref[0:half, :]
-
-    @pl.when(core != 0)
-    def _():
-        pay2_ref[0:half, :] = pay1_ref[half : 2 * half, :]
-
-    shift = qb[...]
-    high = shift.astype(BF16).astype(F32)
-    low = shift - high
+    chans = table.shape[1]
+    bins_count = table.shape[0]
+    moves = [
+        (table, table_v), (pair_gain, pg_v), (wo, wo_v), (qb, qb_v), (wq, own_w.at[0]),
+        (wk, own_w.at[1]), (wv, own_w.at[2]), (wg, own_w.at[3]),
+        (single_gain, sg_v), (token_mask, mask_v), (bias_weight, weight_ref),
+    ]
+    copies = [pltpu.make_async_copy(a, b, sems.at[i]) for i, (a, b) in enumerate(moves)]
+    for c in copies:
+        c.start()
+
+    copies[0].wait()
+    copies[1].wait()
+    eye = (iota((chans, chans), 0) == iota((chans, chans), 1)).astype(F32)
+    emb = table_v[...].astype(F32)
+    emb = emb - jnp.mean(emb, axis=1, keepdims=True)
+    high = emb.astype(BF16).astype(F32)
+    low = emb - high
+    gap = jnp.zeros((48 - bins_count, chans), F32)
+    tail_rows = jnp.zeros((chans - 96, chans), F32)
+    stacked = jnp.concatenate([high, gap, low, gap, tail_rows], axis=0)
+    centre[...] = jnp.concatenate([eye - 1.0 / chans, jnp.transpose(stacked)], axis=1).astype(BF16)
+    gain_t = jnp.transpose(jnp.broadcast_to(pg_v[...].reshape(1, chans), (chans, chans)))
+    gain_b[...] = jnp.concatenate([gain_t, gain_t], axis=1)
+
+    copies[2].wait()
+    copies[3].wait()
+    qb_row = jnp.concatenate([qb_v[...].reshape(1, group), jnp.zeros((1, 128 - group), F32)], axis=1)
+    shift = jnp.transpose(jnp.broadcast_to(qb_row, (128, 128)))[:group]
+    q_high = shift.astype(BF16).astype(F32)
+    q_low = shift - q_high
     lane = iota((group, 128), 1)
 
     def tail(dest):
         pick = (iota((width, 128), 0) - dest * group == iota((width, 128), 1)) & (
             iota((width, 128), 1) < group
         )
-        cut = mm(wo[...], pick.astype(F32).astype(BF16))
-        cut = jnp.where(lane == group, high, cut)
-        cut = jnp.where(lane == group + 1, low, cut)
+        cut = mm(wo_v[...], pick.astype(F32).astype(BF16))
+        cut = jnp.where(lane == group, q_high, cut)
+        cut = jnp.where(lane == group + 1, q_low, cut)
         return cut.astype(BF16)
 
+    base = 4 * tiles * group
+    half = 2 * tiles * group
     pay1_ref[base : base + group, :] = tail(lax.rem(col + 5 - 2 * core, 4))
     pay2_ref[half : half + group, :] = tail(lax.rem(col + 2, 4))
-    own_ref[...] = tail(col)
-
-
-def pack(ids, wq, wk, wv, wg, wo, qb):
+    own_t[...] = tail(col)
+    for c in copies[4:8]:
+        c.wait()
+    for w in range(4):
+        for t in range(tiles):
+            at = (w * tiles + t) * group
+            pay1_ref[at : at + group, :] = own_w[w, :, 128 * t : 128 * t + 128]
+    for w in range(2):
+        for t in range(tiles):
+            at = (w * tiles + t) * group
+            first = own_w[w, :, 128 * t : 128 * t + 128]
+            second = own_w[w + 2, :, 128 * t : 128 * t + 128]
+            pay2_ref[at : at + group, :] = jnp.where(core == 0, first, second)
+    for c in copies[8:]:
+        c.wait()
+    sgain_ref[...] = sg_v[...].reshape(1, width)
+    keys = term_ref.shape[1]
+    terms = (mask_v[...].astype(F32) - 1.0) * 1000000000.0
+    terms = terms.reshape(1, 4 * keys)
+    term = terms[:, :keys]
+    for c in range(1, 4):
+        term = jnp.where(col == c, terms[:, keys * c : keys * (c + 1)], term)
+    term_ref[...] = term
+
+
+def prepare(ids, wq, wk, wv, wg, wo, qb, single_gain, token_mask, table, pair_gain, bias_weight):
     group, width = wq.shape
     tiles = width // 128
+    chans = table.shape[1]
+    tokens = token_mask.shape[0]
+    shape = jax.ShapeDtypeStruct
     return pl.pallas_call(
-        pack_kernel,
-        in_specs=[SMEM] + [VMEM] * 6,
-        out_specs=[VMEM] * 3,
+        prepare_kernel,
+        in_specs=[SMEM] + [HBM] * 11,
+        out_specs=[VMEM] * 9,
         out_shape=[
-            jax.ShapeDtypeStruct(((4 * tiles + 1) * group, 128), BF16),
-            jax.ShapeDtypeStruct(((2 * tiles + 1) * group, 128), BF16),
-            jax.ShapeDtypeStruct((group, 128), BF16),
+            shape(((4 * tiles + 1) * group, 128), BF16),
+            shape(((2 * tiles + 1) * group, 128), BF16),
+            shape((4, group, width), BF16),
+            shape((group, 128), BF16),
+            shape((chans, 2 * chans), BF16),
+            shape((chans, 2 * chans), F32),
+            shape(bias_weight.shape, BF16),
+            shape((1, width), F32),
+            shape((1, tokens // 4), F32),
         ],
-        compiler_params=pltpu.CompilerParams(vmem_limit_bytes=16 * 2**20),
-        cost_estimate=pl.CostEstimate(flops=10**8, bytes_accessed=10**6, transcendentals=0),
-        name="pack_weights",
-    )(ids, wq, wk, wv, wg, wo, qb)
+        scratch_shapes=[
+            pltpu.VMEM(wo.shape, BF16),
+            pltpu.VMEM(qb.shape, F32),
+            pltpu.VMEM(single_gain.shape, F32),
+            pltpu.VMEM(token_mask.shape, jnp.int32),
+            pltpu.VMEM(table.shape, BF16),
+            pltpu.VMEM(pair_gain.shape, F32),
+            pltpu.SemaphoreType.DMA((11,)),
+        ],
+        compiler_params=pltpu.CompilerParams(vmem_limit_bytes=BIG),
+        name="prepare",
+    )(ids, wq, wk, wv, wg, wo, qb, single_gain, token_mask, table, pair_gain, bias_weight)
+
+
+def pair_rows(batch, pair_ref, pair_at, bins_ref, bins_at, centre, gain_b, weight, bias_ref, bias_at):
+    cols = pair_ref.shape[1]
+    sub = iota((48, cols), 0)
+    pad = jnp.zeros((32, cols), BF16)
+    right = []
+    for i in range(batch):
+        bins = bins_ref[bins_at + i : bins_at + i + 1, :]
+        onehot = (sub == bins).astype(F32).astype(BF16)
+        right.append(
+            jnp.concatenate([jnp.transpose(pair_ref[pair_at + i]), onehot, onehot, pad], axis=0)
+        )
+    centred = mm(centre[...], jnp.concatenate(right, axis=1))
+    var = jnp.mean(centred * centred, axis=0, keepdims=True)
+    gain = jnp.concatenate([gain_b[...]] * batch, axis=1)
+    bias = mm(weight[...], (centred * gain).astype(BF16)) * lax.rsqrt(var + EPS)
+    for i in range(batch):
+        bias_ref[bias_at + i] = bias[:, cols * i : cols * (i + 1)].astype(BF16)
+
+
+def pair_kernel(start, batch, pair, bins, centre, gain_b, weight, bias_ref, buf, bins_v, centre_v, gain_v, weight_v, sems):
+    rows = buf.shape[0]
+    parts = rows // batch
+    moves = [
+        (bins.at[start : start + rows], bins_v),
+        (centre, centre_v),
+        (pair.at[start : start + batch], buf.at[0:batch]),
+        (gain_b, gain_v),
+        (weight, weight_v),
+    ]
+    for p in range(1, parts):
+        at = batch * p
+        moves.append((pair.at[start + at : start + at + batch], buf.at[at : at + batch]))
+    copies = [pltpu.make_async_copy(a, b, sems.at[i]) for i, (a, b) in enumerate(moves)]
+    for c in copies:
+        c.start()
+    for c in copies[:5]:
+        c.wait()
+    for p in range(parts):
+        if p:
+            copies[4 + p].wait()
+        at = batch * p
+        pair_rows(batch, buf, at, bins_v, at, centre_v, gain_v, weight_v, bias_ref, at)
+
+
+def pair_bias(pair, bins, centre, gain_b, weight, start, rows, batch=8):
+    cols, chans = pair.shape[1:]
+    heads = weight.shape[0]
+    return pl.pallas_call(
+        functools.partial(pair_kernel, start, batch),
+        in_specs=[HBM] * 5,
+        out_specs=VMEM,
+        out_shape=jax.ShapeDtypeStruct((rows, heads, cols), BF16),
+        scratch_shapes=[
+            pltpu.VMEM((rows, cols, chans), BF16),
+            pltpu.VMEM((rows, cols), jnp.int32),
+            pltpu.VMEM(centre.shape, BF16),
+            pltpu.VMEM(gain_b.shape, F32),
+            pltpu.VMEM(weight.shape, BF16),
+            pltpu.SemaphoreType.DMA((4 + rows // batch,)),
+        ],
+        compiler_params=pltpu.CompilerParams(vmem_limit_bytes=BIG),
+        name="pair_bias",
+    )(pair, bins, centre, gain_b, weight)
 
 
 def attend_kernel(
-    ids, mn, sib, wq, wk, wv, wg, own_t, p1, p2, s1, s2, gain, mask, bias_a, bias_b,
+    ids, mn, sib, own_w, own_t, p1, p2, s1, s2, gain, term, bias_all,
     msg_ref, gate_ref, wo_ref, x_all, w_all,
 ):
     core, col, ylo, rlow = ids[0], ids[1], ids[2], ids[3]
-    group, width = wq.shape
+    group, width = own_w.shape[1:]
     tiles = width // 128
-    heads = bias_a.shape[1]
+    heads = bias_all.shape[1]
     head_dim = width // heads
     tok = 64
     keys = 256
@@ -171,9 +231,8 @@
     before, after, across = lax.rem(col + 3, 4), lax.rem(col + 1, 4), lax.rem(col + 2, 4)
     mine = jnp.where(core == 0, before, after)
     other = jnp.where(core == 0, after, before)
-    own = (wq, wk, wv, wg)
     for w in range(4):
-        w_all[w, pl.ds(pl.multiple_of(col * group, 32), group), :] = own[w][...]
+        w_all[w, pl.ds(pl.multiple_of(col * group, 32), group), :] = own_w[w]
         for t in range(tiles):
             at = (w * tiles + t) * group
             place(mine, w, t, p1[at : at + group, :])
@@ -197,10 +256,15 @@
         for k in range(2):
             block = lax.rem(rlow + 2 * core + 2 * who + k, 4)
             rows = pl.ds(pl.multiple_of(block * tok, tok), tok)
+            at = 2 * tok * k
+            near = [ref[at + tok * q : at + tok * (q + 1), :].astype(F32) for q in range(2)]
+            far = [
+                ref[span + at + tok * q : span + at + tok * (q + 1), :].astype(F32) for q in range(2)
+            ]
             for q in range(2):
-                at = 2 * tok * k + tok * q
-                a = ref[at : at + tok, :].astype(F32)
-                b = ref[span + at : span + at + tok, :].astype(F32)
+                swap = core != who
+                a = jnp.where(swap, near[1 - q], near[q])
+                b = jnp.where(swap, far[1 - q], far[q])
                 x_all[rows, shard * q : shard * q + shard] = jnp.where(ylo == 0, a, b)
                 x_all[rows, shard * (q + 2) : shard * (q + 3)] = jnp.where(ylo == 0, b, a)
     at = 4 * tok
@@ -231,7 +295,7 @@
     lane_w = iota((heads, width), 1)
     head_w = iota((heads, width), 0)
     head_mask = ((lane_w >= head_w * head_dim) & (lane_w < (head_w + 1) * head_dim)).astype(F32)
-    key_term = (mask[pl.ds(col, 1), :].astype(F32) - 1.0) * 1000000000.0
+    key_term = term[...]
     scale = 1.0 / jnp.sqrt(jnp.float32(head_dim))
     part = 16
     rows = part * heads
@@ -241,9 +305,8 @@
     slot = lane_s // heads
     mine_lane = (lane_s % heads) == (iota((rows, 128), 0) % heads)
     for p in range(tok // part):
-        ref = bias_a if p < 2 else bias_b
-        at = part * (p % 2)
-        bias = ref[at : at + part].astype(F32).reshape(rows, keys)
+        at = part * p
+        bias = bias_all[at : at + part].astype(F32).reshape(rows, keys)
         wide = mm(spread, queries[part * p : part * p + part])
         wide = (wide.reshape(part, heads, width) * head_mask[None]).reshape(rows, width).astype(BF16)
         scores = mm_nt(wide, keys_all) * scale + bias + key_term
@@ -263,11 +326,11 @@
         msg_ref[part * p : part * p + part, :] = both.astype(BF16)
 
 
-def attend(ids, mn, sib, wq, wk, wv, wg, own_t, p1, p2, s1, s2, gain, mask, bias_a, bias_b):
-    group, width = wq.shape
+def attend(ids, mn, sib, own_w, own_t, p1, p2, s1, s2, gain, term, bias_all):
+    width = own_w.shape[2]
     return pl.pallas_call(
         attend_kernel,
-        in_specs=[SMEM] + [VMEM] * 15,
+        in_specs=[SMEM] + [VMEM] * 11,
         out_specs=[VMEM] * 3,
         out_shape=[
             jax.ShapeDtypeStruct((64, width + 128), BF16),
@@ -279,9 +342,8 @@
             pltpu.VMEM((4, width, width), BF16),
         ],
         compiler_params=pltpu.CompilerParams(vmem_limit_bytes=24 * 2**20),
-        cost_estimate=pl.CostEstimate(flops=10**9, bytes_accessed=4 * 10**6, transcendentals=300000),
         name="attend",
-    )(ids, mn, sib, wq, wk, wv, wg, own_t, p1, p2, s1, s2, gain, mask, bias_a, bias_b)
+    )(ids, mn, sib, own_w, own_t, p1, p2, s1, s2, gain, term, bias_all)
 
 
 def combine_kernel(m0, m1, m2, m3, gate, wo, out_ref):
@@ -360,35 +422,33 @@
     ids = jnp.stack([core, col, sample // 2, row % 4]).astype(jnp.int32)
     group = query_weight.shape[1]
 
-    wq, wk, wv, wg = (w.T for w in (query_weight, key_weight, value_weight, gate_weight))
-    pay1, pay2, own_t = pack(ids, wq, wk, wv, wg, out_weight, query_bias.reshape(group, 1))
-
     x1 = lax.ppermute(single, "sample", CORE_PAIRS)
-    xa = jnp.concatenate(
-        [jnp.where(core == 0, single, x1), jnp.where(core == 0, x1, single)], axis=0
-    )
+    xa = jnp.concatenate([single, x1], axis=0)
     a0 = lax.ppermute(xa, AXES, long_pairs(0))
     a1 = lax.ppermute(xa, AXES, long_pairs(1))
+
+    xa, token_mask = lax.optimization_barrier((xa, token_mask))
+    wq, wk, wv, wg = (w.T for w in (query_weight, key_weight, value_weight, gate_weight))
+    pay1, pay2, own_w, own_t, centre, gain_b, weight, sgain, term = prepare(
+        ids, wq, wk, wv, wg, out_weight, query_bias, single_gain, token_mask,
+        dist_weight, pair_gain, bias_weight.T,
+    )
     p1 = lax.ppermute(pay1, ("sample", "col"), side_pairs())
     p2 = lax.ppermute(pay2, "col", shift_pairs(2))
 
-    gain = pair_gain.reshape(1, -1)
-    weight_t = bias_weight.T
-    bins = distance_bins[0]
-    bias_a = pair_bias(trunk_pair, bins, dist_weight, gain, weight_t, 0, 32, 8)
-
+    a0, a1, centre = lax.optimization_barrier((a0, a1, centre))
     mine = jnp.concatenate([a0, a1, single], axis=0)
     theirs = lax.ppermute(mine, "sample", YLO_PAIRS)
-    bias_b = pair_bias(trunk_pair, bins, dist_weight, gain, weight_t, 32, 32, 8)
+    bias = pair_bias(
+        trunk_pair, distance_bins[0], centre, gain_b, weight, 0, trunk_pair.shape[0]
+    )
+    theirs, p1, p2, bias = lax.optimization_barrier((theirs, p1, p2, bias))
     mn = jnp.concatenate([mine, theirs], axis=0)
     sib = lax.ppermute(mn, "sample", CORE_PAIRS)
     s1 = lax.ppermute(p1, "sample", CORE_PAIRS)
     s2 = lax.ppermute(p2, "sample", CORE_PAIRS)
 
-    msg, gate, wo = attend(
-        ids, mn, sib, wq, wk, wv, wg, own_t, p1, p2, s1, s2,
-        single_gain.reshape(1, -1), token_mask.reshape(4, -1), bias_a, bias_b,
-    )
+    msg, gate, wo = attend(ids, mn, sib, own_w, own_t, p1, p2, s1, s2, sgain, term, bias)
     others = [lax.ppermute(msg, "col", shift_pairs(k)) for k in (1, 3, 2)]
     update = combine(msg, *others, gate, wo, group)
     return update[None]

time: 69.8 us -> 47.8 us (0.68); the launches traced: 68.4 us -> 47.4 us
  local copies, waits for them, and re-layouts: 12.4 us -> 1.89 us
  waiting for transfers between devices: 12.1 us -> 5.52 us
  Pallas kernels: 20 us -> 14.3 us
  starting transfers between devices: 22.3 us -> 24.2 us
    unnamed x31 -> x18, local copies, waits for them, and re-layouts: 10.2 us -> 1.87 us
    ppermute x1, waiting for transfers between devices: 6 us -> 0.09 us  [body(): p1 = lax.ppermute(pay1, ('sample', 'col'), side_pairs())]
    pallas_call x4 -> x3, Pallas kernels: 18.9 us -> 13.2 us  [the longest x1 6.08 us: pair_bias(): pl.pallas_call(functools.partial(pair_kernel, start, batch), in_specs=[HB...]
    reshape x3 -> x0, local copies, waits for them, and re-layouts: 2.13 us -> none  [the longest x1 0.75 us: body(): query_bias.reshape(group, 1)]
    ppermute x3, starting transfers between devices: 4.6 us -> 6.55 us  [body(): others = [lax.ppermute(msg, 'col', shift_pairs(k)) for k in (1, 3, 2)]]
    ppermute x1, waiting for transfers between devices: 0.01 us -> 1.36 us  [body(): sib = lax.ppermute(mn, 'sample', CORE_PAIRS)]
    ppermute x3, waiting for transfers between devices: 4.71 us -> 3.45 us  [body(): others = [lax.ppermute(msg, 'col', shift_pairs(k)) for k in (1, 3, 2)]]
    ppermute x1, waiting for transfers between devices: 1.39 us -> 0.6 us  [body(): x1 = lax.ppermute(single, 'sample', CORE_PAIRS)]
  transfers between devices with their start and end apart: 12 -> 12, of which waited for: 5 -> 6; matrix products, arithmetic and copies ran while one was open for 5% -> 5% of each run, Pallas kernels for 22% -> 19%
where the time goes in v2:
time: 47.8 us; the launch traced here: 47.4 us
  starting transfers between devices  24.2 us (51%)
  Pallas kernels  14.3 us (30%)
  waiting for transfers between devices  5.52 us (12%)
  local copies, waits for them, and re-layouts  1.89 us (4%)
  other arithmetic  1.33 us (3%)
    ppermute x1, starting transfers between devices, body(): p2 = lax.ppermute(pay2, 'col', shift_pairs(2))  11.2 us
    ppermute x3, starting transfers between devices, body(): others = [lax.ppermute(msg, 'col', shift_pairs(k)) for k in (1, 3, 2)]  6.55 us
    pallas_call x1, Pallas kernels, pair_bias(): pl.pallas_call(functools.partial(pair_kernel, start, batch), in_specs=[HB...  6.08 us
    pallas_call x1, Pallas kernels, attend(): pl.pallas_call(attend_kernel, in_specs=[SMEM] + [VMEM] * 11, out_specs=[V...  4.07 us
    ppermute x1, starting transfers between devices, body(): a1 = lax.ppermute(xa, AXES, long_pairs(1))  3.65 us
    ppermute x3, waiting for transfers between devices, body(): others = [lax.ppermute(msg, 'col', shift_pairs(k)) for k in (1, 3, 2)]  3.45 us
    pallas_call x1, Pallas kernels, prepare(): pl.pallas_call(prepare_kernel, in_specs=[SMEM] + [HBM] * 11, out_specs=[V...  3.04 us
    unnamed x18, local copies, waits for them, and re-layouts  1.87 us
  transfers between devices with their start and end apart: 12, of which 6 were waited for; matrix products, arithmetic and copies ran while one was open for 5% of the time, Pallas kernels for 19%

profile of v2, /device:TPU:8, one launch (start us, length us, event | category | flops | bytes accessed | tf_op | source)
XLA Modules:
  0.0 47.4 jit_solution(3284041413633792265)
XLA Ops:
  0.0 0.8 %constant_dynamic-update-slice_fusion.1 = bf16[128,96]{1,0:T(8,128)(2,1)S(1)} fusion(bf16[64,96]{1,0:T(8,128)(2,1)} %param.17), kind=kLoop, calls=%fused_computation.2 | loop fusion | bytes 28672
  0.8 0.6 %collective-permute-done = bf16[64,96]{1,0:T(8,128)(2,1)S(1)} collective-permute-done((bf16[64,96]{1,0:T(8,128)(2,1)}, bf16[64,96]{1,0:T(8,128)(2,1)S(1)}, u32[]{:S(2)}, u32[]{:S(2)}) %collective-permute-start) | collective-permute-done | bytes 12320 | tf_op jit(solution)/shard_map/ppermute | solution.py:425
  1.4 3.6 %collective-permute-start.2 = (bf16[128,96]{1,0:T(8,128)(2,1)S(1)}, bf16[128,96]{1,0:T(8,128)(2,1)S(1)}, u32[]{:S(2)}, u32[]{:S(2)}) collective-permute-start(bf16[128,96]{1,0:T(8,128)(2,1)S(1)} %constant_dynamic-update-slice_fusion), channel_id=1, source_target_pairs={{4,0},{20,1},{36,2},{52,3},{8,4},{24,5},{40,6},{56,7},{12,8},{28,9... | collective-permute-start | bytes 73736 | tf_op jit(solution)/shard_map/ppermute | solution.py:428
  5.1 0.7 %collective-permute-start.1 = (bf16[128,96]{1,0:T(8,128)(2,1)S(1)}, bf16[128,96]{1,0:T(8,128)(2,1)S(1)}, u32[]{:S(2)}, u32[]{:S(2)}) collective-permute-start(bf16[128,96]{1,0:T(8,128)(2,1)S(1)} %constant_dynamic-update-slice_fusion), channel_id=1, source_target_pairs={{0,0},{16,1},{32,2},{48,3},{4,4},{20,5},{36,6},{52,7},{8,8},{24,9}... | collective-permute-start | bytes 73736 | tf_op jit(solution)/shard_map/ppermute | solution.py:427
  5.7 0.6 %pad_add_fusion.ids = s32[4]{0:T(128)} fusion(s32[1]{0:T(128)} %bitcast.3, s32[1]{0:T(128)} %bitcast.2, s32[1]{0:T(128)} %bitcast.1, s32[1]{0:T(128)} %bitcast), kind=kLoop, calls=%fused_computation.7 | loop fusion | flops 12 | bytes 32 | tf_op jit(solution)/shard_map/stack | solution.py:422
  6.3 3.0 %prepare.1 = (bf16[1248,128]{1,0:T(8,128)(2,1)}, bf16[672,128]{1,0:T(8,128)(2,1)}, bf16[4,96,384]{2,1,0:T(8,128)(2,1)}, bf16[96,128]{1,0:T(8,128)(2,1)}, bf16[12...) custom-call(s32[4]{0:T(128)} %pad_add_fusion.ids, ...), custom_call_target="tpu_custom_call" | custom-call | tf_op jit(solution)/shard_map/prepare/pallas_call | solution.py:118
  9.4 11.2 %collective-permute-start.5 = (bf16[672,128]{1,0:T(8,128)(2,1)}, bf16[672,128]{1,0:T(8,128)(2,1)S(1)}, u32[]{:S(2)}, u32[]{:S(2)}) collective-permute-start(bf16[672,128]{1,0:T(8,128)(2,1)} %get-tuple-element.30), channel_id=1, source_target_pairs={{0,2},{1,3},{2,0},{3,1},{4,6},{5,7},{6,4},{7,5},{8,10},{9,11},{10,... | collective-permute-start | bytes 516104 | tf_op jit(solution)/shard_map/ppermute | solution.py:437
  20.6 0.0 collective-permute-start.4
  20.7 0.7 %pad_maximum_fusion = bf16[320,96]{1,0:T(8,128)(2,1)S(1)} fusion(bf16[64,96]{1,0:T(8,128)(2,1)} %param.17, bf16[128,96]{1,0:T(8,128)(2,1)S(1)} %collective-permute-done.2, bf16[128,96]{1,0:T(8,128)(2,1)S(1)} %collective-permute-done.1), kind=kLoop, calls=%fused_computation | loop fusion | flops 184320 | bytes 122880 | tf_op jit(solution)/shard_map/concatenate | solution.py:440
  21.4 1.4 %collective-permute-start.3 = (bf16[320,96]{1,0:T(8,128)(2,1)S(1)}, bf16[320,96]{1,0:T(8,128)(2,1)S(1)}, u32[]{:S(2)}, u32[]{:S(2)}) collective-permute-start(bf16[320,96]{1,0:T(8,128)(2,1)S(1)} %pad_maximum_fusion), channel_id=1, source_target_pairs={{0,128},{64,192},{128,0},{192,64},{1,129},{65,193},{129,1},{193,65... | collective-permute-start | bytes 184328 | tf_op jit(solution)/shard_map/ppermute | solution.py:441
  22.8 6.1 %pair_bias.1.bias_all = bf16[64,16,256]{2,1,0:T(8,128)(2,1)} custom-call(bf16[64,256,128]{2,1,0:T(8,128)(2,1)} %pair.1, s32[64,256]{1,0:T(8,128)} %bitcast.15, bf16[128,256]{1,0:T(8,128)(2,1)} %get-tuple-element.31.centre, f32[128,256]{1,0:T(8,128)} %get-tuple-element.32.gain_b, bf16[16,128]{1,0:T(8,128)(2,1)} %get-tuple-element.33.weight), custom_call_target="tpu_custom_call" | custom-call | tf_op jit(solution)/shard_map/pair_bias/pallas_call | solution.py:194
  29.0 0.1 collective-permute-done.4.p1
  29.0 0.0 collective-permute-start.7
  29.1 0.5 %collective-permute-start.8 = (bf16[672,128]{1,0:T(8,128)(2,1)S(1)}, bf16[672,128]{1,0:T(8,128)(2,1)S(1)}, u32[]{:S(2)}, u32[]{:S(2)}) collective-permute-start(bf16[672,128]{1,0:T(8,128)(2,1)S(1)} %collective-permute-done.5.p2), channel_id=1, source_target_pairs={{0,64},{64,0},{128,192},{192,128},{1,65},{65,1},{129,193},{193,129... | collective-permute-start | bytes 516104 | tf_op jit(solution)/shard_map/ppermute | solution.py:449
  29.6 0.2 collective-permute-start.6
  29.8 1.4 %collective-permute-done.6.sib = bf16[640,96]{1,0:T(8,128)(2,1)S(1)} collective-permute-done((bf16[640,96]{1,0:T(8,128)(2,1)S(1)}, bf16[640,96]{1,0:T(8,128)(2,1)S(1)}, u32[]{:S(2)}, u32[]{:S(2)}) %collective-permute-start.6) | collective-permute-done | bytes 122912 | tf_op jit(solution)/shard_map/ppermute | solution.py:447
  31.2 1.0 %copy-done = bf16[64,16,256]{2,1,0:T(8,128)(2,1)S(1)} copy-done((bf16[64,16,256]{2,1,0:T(8,128)(2,1)S(1)}, bf16[64,16,256]{2,1,0:T(8,128)(2,1)}, u32[]{:S(2)}) %copy-start) | copy-done | bytes 524312
  32.2 4.1 %attend.1 = (bf16[64,512]{1,0:T(8,128)(2,1)S(1)}, f32[64,384]{1,0:T(8,128)S(1)}, bf16[384,128]{1,0:T(8,128)(2,1)S(1)}) custom-call(s32[4]{0:T(128)S(1)} %copy-done.3, bf16[640,96]{1,0:T(8,128)(2,1)S(1)} %constant_dynamic-update-slice_fusion.2.mn, bf16[640,96]{1,0:T(8,128)(2,1)S(1)} %collective-permute-done.6.sib, bf16[4,96,384]{2,1,0:T(8,128)(2,1)S(1)} %copy-done.1, ...), custom_call_target="tpu_custom_call" | custom-call | tf_op jit(solution)/shard_map/attend/pallas_call | solution.py:331
  36.3 4.5 %collective-permute-start.11 = (bf16[64,512]{1,0:T(8,128)(2,1)S(1)}, bf16[64,512]{1,0:T(8,128)(2,1)S(1)}, u32[]{:S(2)}, u32[]{:S(2)}) collective-permute-start(bf16[64,512]{1,0:T(8,128)(2,1)S(1)} %get-tuple-element.42.m0), channel_id=1, source_target_pairs={{0,2},{1,3},{2,0},{3,1},{4,6},{5,7},{6,4},{7,5},{8,10},{9,11},{10,... | collective-permute-start | bytes 196616 | tf_op jit(solution)/shard_map/ppermute | solution.py:452
  40.8 2.0 %collective-permute-start.9 = (bf16[64,512]{1,0:T(8,128)(2,1)S(1)}, bf16[64,512]{1,0:T(8,128)(2,1)S(1)}, u32[]{:S(2)}, u32[]{:S(2)}) collective-permute-start(bf16[64,512]{1,0:T(8,128)(2,1)S(1)} %get-tuple-element.42.m0), channel_id=1, source_target_pairs={{0,1},{1,2},{2,3},{3,0},{4,5},{5,6},{6,7},{7,4},{8,9},{9,10},{10,1... | collective-permute-start | bytes 196616 | tf_op jit(solution)/shard_map/ppermute | solution.py:452
  42.9 0.4 collective-permute-done.11.m3
  43.2 1.9 %collective-permute-done.10.m2 = bf16[64,512]{1,0:T(8,128)(2,1)S(1)} collective-permute-done((bf16[64,512]{1,0:T(8,128)(2,1)S(1)}, bf16[64,512]{1,0:T(8,128)(2,1)S(1)}, u32[]{:S(2)}, u32[]{:S(2)}) %collective-permute-start.10) | collective-permute-done | bytes 65568 | tf_op jit(solution)/shard_map/ppermute | solution.py:452
  45.1 1.2 %collective-permute-done.9.m1 = bf16[64,512]{1,0:T(8,128)(2,1)S(1)} collective-permute-done((bf16[64,512]{1,0:T(8,128)(2,1)S(1)}, bf16[64,512]{1,0:T(8,128)(2,1)S(1)}, u32[]{:S(2)}, u32[]{:S(2)}) %collective-permute-start.9) | collective-permute-done | bytes 65568 | tf_op jit(solution)/shard_map/ppermute | solution.py:452
  46.3 1.1 %combine.1 = bf16[64,96]{1,0:T(8,128)(2,1)} custom-call(bf16[64,512]{1,0:T(8,128)(2,1)S(1)} %get-tuple-element.42.m0, bf16[64,512]{1,0:T(8,128)(2,1)S(1)} %collective-permute-done.9.m1, bf16[64,512]{1,0:T(8,128)(2,1)S(1)} %collective-permute-done.10.m2, bf16[64,512]{1,0:T(8,128)(2,1)S(1)} %collective-permute-done.11.m3, ...), custom_call_target="tpu_custom_call" | custom-call | tf_op jit(solution)/shard_map/combine/pallas_call | solution.py:377
  (26 shorter events, 0.1 us)
Async XLA Ops:
  0.0 29.1 %copy-start.6 = (bf16[64,96]{1,0:T(8,128)(2,1)S(1)}, bf16[64,96]{1,0:T(8,128)(2,1)}, u32[]{:S(2)}) copy-start(bf16[64,96]{1,0:T(8,128)(2,1)} %param.17) | copy-start | bytes 36868
  0.0 1.4 %collective-permute-start = (bf16[64,96]{1,0:T(8,128)(2,1)}, bf16[64,96]{1,0:T(8,128)(2,1)S(1)}, u32[]{:S(2)}, u32[]{:S(2)}) collective-permute-start(bf16[64,96]{1,0:T(8,128)(2,1)} %param.17), channel_id=1, source_target_pairs={{0,64},{64,0},{128,192},{192,128},{1,65},{65,1},{129,193},{193,129... | collective-permute-start | bytes 36872 | tf_op jit(solution)/shard_map/ppermute | solution.py:425
  1.4 19.2 %collective-permute-start.2 = (bf16[128,96]{1,0:T(8,128)(2,1)S(1)}, bf16[128,96]{1,0:T(8,128)(2,1)S(1)}, u32[]{:S(2)}, u32[]{:S(2)}) collective-permute-start(bf16[128,96]{1,0:T(8,128)(2,1)S(1)} %constant_dynamic-update-slice_fusion), channel_id=1, source_target_pairs={{4,0},{20,1},{36,2},{52,3},{8,4},{24,5},{40,6},{56,7},{12,8},{28,9... | collective-permute-start | bytes 73736 | tf_op jit(solution)/shard_map/ppermute | solution.py:428
  5.1 15.6 %collective-permute-start.1 = (bf16[128,96]{1,0:T(8,128)(2,1)S(1)}, bf16[128,96]{1,0:T(8,128)(2,1)S(1)}, u32[]{:S(2)}, u32[]{:S(2)}) collective-permute-start(bf16[128,96]{1,0:T(8,128)(2,1)S(1)} %constant_dynamic-update-slice_fusion), channel_id=1, source_target_pairs={{0,0},{16,1},{32,2},{48,3},{4,4},{20,5},{36,6},{52,7},{8,8},{24,9}... | collective-permute-start | bytes 73736 | tf_op jit(solution)/shard_map/ppermute | solution.py:427
  6.3 24.9 %copy-start.3 = (s32[4]{0:T(128)S(1)}, s32[4]{0:T(128)}, u32[]{:S(2)}) copy-start(s32[4]{0:T(128)} %pad_add_fusion.ids) | copy-start | bytes 52
  9.4 21.8 %copy-start.1 = (bf16[4,96,384]{2,1,0:T(8,128)(2,1)S(1)}, bf16[4,96,384]{2,1,0:T(8,128)(2,1)}, u32[]{:S(2)}) copy-start(bf16[4,96,384]{2,1,0:T(8,128)(2,1)} %get-tuple-element.35.own_w) | copy-start | bytes 884740
  9.4 21.8 %copy-start.2 = (bf16[96,128]{1,0:T(8,128)(2,1)S(1)}, bf16[96,128]{1,0:T(8,128)(2,1)}, u32[]{:S(2)}) copy-start(bf16[96,128]{1,0:T(8,128)(2,1)} %get-tuple-element.36.own_t) | copy-start | bytes 73732
  9.4 21.8 %copy-start.4 = (f32[1,384]{1,0:T(1,128)S(1)}, f32[1,384]{1,0:T(1,128)}, u32[]{:S(2)}) copy-start(f32[1,384]{1,0:T(1,128)} %get-tuple-element.39.gain) | copy-start | bytes 4612
  9.4 21.8 %copy-start.5 = (f32[1,256]{1,0:T(1,128)S(1)}, f32[1,256]{1,0:T(1,128)}, u32[]{:S(2)}) copy-start(f32[1,256]{1,0:T(1,128)} %get-tuple-element.40.term) | copy-start | bytes 3076
  9.4 19.5 %collective-permute-start.5 = (bf16[672,128]{1,0:T(8,128)(2,1)}, bf16[672,128]{1,0:T(8,128)(2,1)S(1)}, u32[]{:S(2)}, u32[]{:S(2)}) collective-permute-start(bf16[672,128]{1,0:T(8,128)(2,1)} %get-tuple-element.30), channel_id=1, source_target_pairs={{0,2},{1,3},{2,0},{3,1},{4,6},{5,7},{6,4},{7,5},{8,10},{9,11},{10,... | collective-permute-start | bytes 516104 | tf_op jit(solution)/shard_map/ppermute | solution.py:437
  20.6 8.4 %collective-permute-start.4 = (bf16[1248,128]{1,0:T(8,128)(2,1)}, bf16[1248,128]{1,0:T(8,128)(2,1)S(1)}, u32[]{:S(2)}, u32[]{:S(2)}) collective-permute-start(bf16[1248,128]{1,0:T(8,128)(2,1)} %get-tuple-element.29), channel_id=1, source_target_pairs={{0,1},{1,2},{2,3},{3,0},{64,67},{65,64},{66,65},{67,66},{128,129},... | collective-permute-start | bytes 958472 | tf_op jit(solution)/shard_map/ppermute | solution.py:436
  21.4 7.5 %collective-permute-start.3 = (bf16[320,96]{1,0:T(8,128)(2,1)S(1)}, bf16[320,96]{1,0:T(8,128)(2,1)S(1)}, u32[]{:S(2)}, u32[]{:S(2)}) collective-permute-start(bf16[320,96]{1,0:T(8,128)(2,1)S(1)} %pad_maximum_fusion), channel_id=1, source_target_pairs={{0,128},{64,192},{128,0},{192,64},{1,129},{65,193},{129,1},{193,65... | collective-permute-start | bytes 184328 | tf_op jit(solution)/shard_map/ppermute | solution.py:441
  29.0 2.1 %collective-permute-start.7 = (bf16[1248,128]{1,0:T(8,128)(2,1)S(1)}, bf16[1248,128]{1,0:T(8,128)(2,1)S(1)}, u32[]{:S(2)}, u32[]{:S(2)}) collective-permute-start(bf16[1248,128]{1,0:T(8,128)(2,1)S(1)} %collective-permute-done.4.p1), channel_id=1, source_target_pairs={{0,64},{64,0},{128,192},{192,128},{1,65},{65,1},{129,193},{193,129... | collective-permute-start | bytes 958472 | tf_op jit(solution)/shard_map/ppermute | solution.py:448
  29.1 2.1 %collective-permute-start.8 = (bf16[672,128]{1,0:T(8,128)(2,1)S(1)}, bf16[672,128]{1,0:T(8,128)(2,1)S(1)}, u32[]{:S(2)}, u32[]{:S(2)}) collective-permute-start(bf16[672,128]{1,0:T(8,128)(2,1)S(1)} %collective-permute-done.5.p2), channel_id=1, source_target_pairs={{0,64},{64,0},{128,192},{192,128},{1,65},{65,1},{129,193},{193,129... | collective-permute-start | bytes 516104 | tf_op jit(solution)/shard_map/ppermute | solution.py:449
  29.6 1.6 %collective-permute-start.6 = (bf16[640,96]{1,0:T(8,128)(2,1)S(1)}, bf16[640,96]{1,0:T(8,128)(2,1)S(1)}, u32[]{:S(2)}, u32[]{:S(2)}) collective-permute-start(bf16[640,96]{1,0:T(8,128)(2,1)S(1)} %constant_dynamic-update-slice_fusion.2.mn), channel_id=1, source_target_pairs={{0,64},{64,0},{128,192},{192,128},{1,65},{65,1},{129,193},{193,129... | collective-permute-start | bytes 368648 | tf_op jit(solution)/shard_map/ppermute | solution.py:447
  31.2 1.0 %copy-start = (bf16[64,16,256]{2,1,0:T(8,128)(2,1)S(1)}, bf16[64,16,256]{2,1,0:T(8,128)(2,1)}, u32[]{:S(2)}) copy-start(bf16[64,16,256]{2,1,0:T(8,128)(2,1)} %pair_bias.1.bias_all) | copy-start | bytes 1572868
  36.3 6.9 %collective-permute-start.11 = (bf16[64,512]{1,0:T(8,128)(2,1)S(1)}, bf16[64,512]{1,0:T(8,128)(2,1)S(1)}, u32[]{:S(2)}, u32[]{:S(2)}) collective-permute-start(bf16[64,512]{1,0:T(8,128)(2,1)S(1)} %get-tuple-element.42.m0), channel_id=1, source_target_pairs={{0,2},{1,3},{2,0},{3,1},{4,6},{5,7},{6,4},{7,5},{8,10},{9,11},{10,... | collective-permute-start | bytes 196616 | tf_op jit(solution)/shard_map/ppermute | solution.py:452
  40.8 4.3 %collective-permute-start.10 = (bf16[64,512]{1,0:T(8,128)(2,1)S(1)}, bf16[64,512]{1,0:T(8,128)(2,1)S(1)}, u32[]{:S(2)}, u32[]{:S(2)}) collective-permute-start(bf16[64,512]{1,0:T(8,128)(2,1)S(1)} %get-tuple-element.42.m0), channel_id=1, source_target_pairs={{0,3},{1,0},{2,1},{3,2},{4,7},{5,4},{6,5},{7,6},{8,11},{9,8},{10,9... | collective-permute-start | bytes 196616 | tf_op jit(solution)/shard_map/ppermute | solution.py:452
  40.8 5.5 %collective-permute-start.9 = (bf16[64,512]{1,0:T(8,128)(2,1)S(1)}, bf16[64,512]{1,0:T(8,128)(2,1)S(1)}, u32[]{:S(2)}, u32[]{:S(2)}) collective-permute-start(bf16[64,512]{1,0:T(8,128)(2,1)S(1)} %get-tuple-element.42.m0), channel_id=1, source_target_pairs={{0,1},{1,2},{2,3},{3,0},{4,5},{5,6},{6,7},{7,4},{8,9},{9,10},{10,1... | collective-permute-start | bytes 196616 | tf_op jit(solution)/shard_map/ppermute | solution.py:452

commit v3 on v2

--- a/solution.py
+++ b/solution.py
@@ -13,7 +13,6 @@
 EPS = 1e-05
 BIG = 58 * 2**20
 VMEM = pl.BlockSpec(memory_space=pltpu.VMEM)
-SMEM = pl.BlockSpec(memory_space=pltpu.SMEM)
 HBM = pl.BlockSpec(memory_space=pltpu.HBM)
 AXES = ("sample", "row", "col")
 
@@ -31,11 +30,11 @@
 
 
 def prepare_kernel(
-    ids, wq, wk, wv, wg, wo, qb, single_gain, token_mask, table, pair_gain, bias_weight,
+    wq, wk, wv, wg, wo, qb, single_gain, token_mask, table, pair_gain, bias_weight,
     pay1_ref, pay2_ref, own_w, own_t, centre, gain_b, weight_ref, sgain_ref, term_ref,
     wo_v, qb_v, sg_v, mask_v, table_v, pg_v, sems,
 ):
-    core, col = ids[0], ids[1]
+    core, col = lax.rem(lax.axis_index("sample"), 2), lax.axis_index("col")
     group, width = wq.shape
     tiles = width // 128
     chans = table.shape[1]
@@ -109,7 +108,7 @@
     term_ref[...] = term
 
 
-def prepare(ids, wq, wk, wv, wg, wo, qb, single_gain, token_mask, table, pair_gain, bias_weight):
+def prepare(wq, wk, wv, wg, wo, qb, single_gain, token_mask, table, pair_gain, bias_weight):
     group, width = wq.shape
     tiles = width // 128
     chans = table.shape[1]
@@ -117,7 +116,7 @@
     shape = jax.ShapeDtypeStruct
     return pl.pallas_call(
         prepare_kernel,
-        in_specs=[SMEM] + [HBM] * 11,
+        in_specs=[HBM] * 11,
         out_specs=[VMEM] * 9,
         out_shape=[
             shape(((4 * tiles + 1) * group, 128), BF16),
@@ -141,7 +140,7 @@
         ],
         compiler_params=pltpu.CompilerParams(vmem_limit_bytes=BIG),
         name="prepare",
-    )(ids, wq, wk, wv, wg, wo, qb, single_gain, token_mask, table, pair_gain, bias_weight)
+    )(wq, wk, wv, wg, wo, qb, single_gain, token_mask, table, pair_gain, bias_weight)
 
 
 def pair_rows(batch, pair_ref, pair_at, bins_ref, bins_at, centre, gain_b, weight, bias_ref, bias_at):
@@ -163,57 +162,45 @@
         bias_ref[bias_at + i] = bias[:, cols * i : cols * (i + 1)].astype(BF16)
 
 
-def pair_kernel(start, batch, pair, bins, centre, gain_b, weight, bias_ref, buf, bins_v, centre_v, gain_v, weight_v, sems):
+def pair_kernel(batch, pair, bins, centre, gain_b, weight, bias_ref, buf, sems):
     rows = buf.shape[0]
-    parts = rows // batch
-    moves = [
-        (bins.at[start : start + rows], bins_v),
-        (centre, centre_v),
-        (pair.at[start : start + batch], buf.at[0:batch]),
-        (gain_b, gain_v),
-        (weight, weight_v),
-    ]
-    for p in range(1, parts):
-        at = batch * p
-        moves.append((pair.at[start + at : start + at + batch], buf.at[at : at + batch]))
-    copies = [pltpu.make_async_copy(a, b, sems.at[i]) for i, (a, b) in enumerate(moves)]
+    copies = []
+    for p in range(rows // batch):
+        span = pl.ds(batch * p, batch)
+        copies.append(pltpu.make_async_copy(pair.at[span], buf.at[span], sems.at[p]))
     for c in copies:
         c.start()
-    for c in copies[:5]:
+    for p, c in enumerate(copies):
         c.wait()
-    for p in range(parts):
-        if p:
-            copies[4 + p].wait()
         at = batch * p
-        pair_rows(batch, buf, at, bins_v, at, centre_v, gain_v, weight_v, bias_ref, at)
-
-
-def pair_bias(pair, bins, centre, gain_b, weight, start, rows, batch=8):
-    cols, chans = pair.shape[1:]
+        pair_rows(batch, buf, at, bins, at, centre, gain_b, weight, bias_ref, at)
+
+
+def pair_bias(pair, bins, centre, gain_b, weight, batch=16):
+    rows, cols, chans = pair.shape
     heads = weight.shape[0]
     return pl.pallas_call(
-        functools.partial(pair_kernel, start, batch),
-        in_specs=[HBM] * 5,
+        functools.partial(pair_kernel, batch),
+        in_specs=[HBM] + [VMEM] * 4,
         out_specs=VMEM,
         out_shape=jax.ShapeDtypeStruct((rows, heads, cols), BF16),
         scratch_shapes=[
             pltpu.VMEM((rows, cols, chans), BF16),
-            pltpu.VMEM((rows, cols), jnp.int32),
-            pltpu.VMEM(centre.shape, BF16),
-            pltpu.VMEM(gain_b.shape, F32),
-            pltpu.VMEM(weight.shape, BF16),
-            pltpu.SemaphoreType.DMA((4 + rows // batch,)),
+            pltpu.SemaphoreType.DMA((rows // batch,)),
         ],
-        compiler_params=pltpu.CompilerParams(vmem_limit_bytes=BIG),
+        compiler_params=pltpu.CompilerParams(vmem_limit_bytes=53 * 2**20),
         name="pair_bias",
     )(pair, bins, centre, gain_b, weight)
 
 
 def attend_kernel(
-    ids, mn, sib, own_w, own_t, p1, p2, s1, s2, gain, term, bias_all,
+    mn, sib, own_w, own_t, p1, p2, s1, s2, gain, term, bias_all,
     msg_ref, gate_ref, wo_ref, x_all, w_all,
 ):
-    core, col, ylo, rlow = ids[0], ids[1], ids[2], ids[3]
+    sample = lax.axis_index("sample")
+    core, ylo = lax.rem(sample, 2), sample // 2
+    col = lax.axis_index("col")
+    rlow = lax.rem(lax.axis_index("row"), 4)
     group, width = own_w.shape[1:]
     tiles = width // 128
     heads = bias_all.shape[1]
@@ -254,13 +241,17 @@
     shard = mn.shape[1]
     for who, ref in ((0, mn), (1, sib)):
         for k in range(2):
-            block = lax.rem(rlow + 2 * core + 2 * who + k, 4)
+            side = core if who == 0 else 1 - core
+            zlow, yhigh = rlow // 2, lax.rem(rlow, 2)
+            block = 2 * lax.rem(zlow + side, 2) + lax.rem(yhigh + k, 2)
             rows = pl.ds(pl.multiple_of(block * tok, tok), tok)
             at = 2 * tok * k
             near = [ref[at + tok * q : at + tok * (q + 1), :].astype(F32) for q in range(2)]
             far = [
                 ref[span + at + tok * q : span + at + tok * (q + 1), :].astype(F32) for q in range(2)
             ]
+            if k == 1:
+                near, far = far, near
             for q in range(2):
                 swap = core != who
                 a = jnp.where(swap, near[1 - q], near[q])
@@ -297,7 +288,7 @@
     head_mask = ((lane_w >= head_w * head_dim) & (lane_w < (head_w + 1) * head_dim)).astype(F32)
     key_term = term[...]
     scale = 1.0 / jnp.sqrt(jnp.float32(head_dim))
-    part = 16
+    part = 64
     rows = part * heads
     spread = (iota((rows, part), 0) // heads == iota((rows, part), 1)).astype(F32).astype(BF16)
     gather = (iota((part, rows), 1) // heads == iota((part, rows), 0)).astype(F32).astype(BF16)
@@ -313,7 +304,7 @@
         top = jnp.max(scores, axis=1, keepdims=True)
         weights = jnp.exp(scores - top)
         total = jnp.sum(weights, axis=1, keepdims=True)
-        out = mm(weights.astype(BF16), values_all) / total
+        out = mm(weights.astype(BF16), values_all) * (1.0 / total)
         out = (out.reshape(part, heads, width) * head_mask[None]).reshape(rows, width).astype(BF16)
         t1 = top.astype(BF16).astype(F32)
         t2 = (top - t1).astype(BF16).astype(F32)
@@ -326,11 +317,11 @@
         msg_ref[part * p : part * p + part, :] = both.astype(BF16)
 
 
-def attend(ids, mn, sib, own_w, own_t, p1, p2, s1, s2, gain, term, bias_all):
+def attend(mn, sib, own_w, own_t, p1, p2, s1, s2, gain, term, bias_all):
     width = own_w.shape[2]
     return pl.pallas_call(
         attend_kernel,
-        in_specs=[SMEM] + [VMEM] * 11,
+        in_specs=[VMEM] * 11,
         out_specs=[VMEM] * 3,
         out_shape=[
             jax.ShapeDtypeStruct((64, width + 128), BF16),
@@ -343,7 +334,7 @@
         ],
         compiler_params=pltpu.CompilerParams(vmem_limit_bytes=24 * 2**20),
         name="attend",
-    )(ids, mn, sib, own_w, own_t, p1, p2, s1, s2, gain, term, bias_all)
+    )(mn, sib, own_w, own_t, p1, p2, s1, s2, gain, term, bias_all)
 
 
 def combine_kernel(m0, m1, m2, m3, gate, wo, out_ref):
@@ -394,7 +385,8 @@
         for rb in range(4):
             for rl in range(4):
                 for c in range(4):
-                    source = device(s, 4 * c + (rl + 2 * (s % 2) + k) % 4, rb)
+                    near = rl ^ (2 * (s % 2)) ^ k
+                    source = device(s ^ (2 * k), 4 * c + near, (rb + 2) % 4)
                     pairs.append((source, device(s, 4 * rb + rl, c)))
     return pairs
 
@@ -415,11 +407,6 @@
     trunk_pair, distance_bins, token_mask, single, dist_weight, pair_gain, bias_weight,
     single_gain, query_weight, query_bias, key_weight, value_weight, gate_weight, out_weight,
 ):
-    sample = lax.axis_index("sample")
-    row = lax.axis_index("row")
-    col = lax.axis_index("col")
-    core = sample % 2
-    ids = jnp.stack([core, col, sample // 2, row % 4]).astype(jnp.int32)
     group = query_weight.shape[1]
 
     x1 = lax.ppermute(single, "sample", CORE_PAIRS)
@@ -430,25 +417,23 @@
     xa, token_mask = lax.optimization_barrier((xa, token_mask))
     wq, wk, wv, wg = (w.T for w in (query_weight, key_weight, value_weight, gate_weight))
     pay1, pay2, own_w, own_t, centre, gain_b, weight, sgain, term = prepare(
-        ids, wq, wk, wv, wg, out_weight, query_bias, single_gain, token_mask,
+        wq, wk, wv, wg, out_weight, query_bias, single_gain, token_mask,
         dist_weight, pair_gain, bias_weight.T,
     )
+    a0, a1, pay1, pay2, centre = lax.optimization_barrier((a0, a1, pay1, pay2, centre))
     p1 = lax.ppermute(pay1, ("sample", "col"), side_pairs())
     p2 = lax.ppermute(pay2, "col", shift_pairs(2))
 
-    a0, a1, centre = lax.optimization_barrier((a0, a1, centre))
-    mine = jnp.concatenate([a0, a1, single], axis=0)
+    mine = jnp.concatenate([a0, a1, xa[: single.shape[0]]], axis=0)
     theirs = lax.ppermute(mine, "sample", YLO_PAIRS)
-    bias = pair_bias(
-        trunk_pair, distance_bins[0], centre, gain_b, weight, 0, trunk_pair.shape[0]
-    )
+    bias = pair_bias(trunk_pair, distance_bins[0], centre, gain_b, weight)
     theirs, p1, p2, bias = lax.optimization_barrier((theirs, p1, p2, bias))
     mn = jnp.concatenate([mine, theirs], axis=0)
     sib = lax.ppermute(mn, "sample", CORE_PAIRS)
     s1 = lax.ppermute(p1, "sample", CORE_PAIRS)
     s2 = lax.ppermute(p2, "sample", CORE_PAIRS)
 
-    msg, gate, wo = attend(ids, mn, sib, own_w, own_t, p1, p2, s1, s2, sgain, term, bias)
+    msg, gate, wo = attend(mn, sib, own_w, own_t, p1, p2, s1, s2, sgain, term, bias)
     others = [lax.ppermute(msg, "col", shift_pairs(k)) for k in (1, 3, 2)]
     update = combine(msg, *others, gate, wo, group)
     return update[None]

time: 47.8 us -> 43.3 us (0.906)
  Pallas kernels: 14.3 us -> 10.3 us
  starting transfers between devices: 24.2 us -> 20.5 us
  waiting for transfers between devices: 5.52 us -> 8.05 us
  local copies, waits for them, and re-layouts: 1.89 us -> 4.01 us
  other arithmetic: 1.33 us -> 0.05 us
    ppermute x1, starting transfers between devices: 11.2 us -> 1.4 us  [body(): p2 = lax.ppermute(pay2, 'col', shift_pairs(2))]
    ppermute x1, starting transfers between devices: 3.65 us -> 8.2 us  [body(): a1 = lax.ppermute(xa, AXES, long_pairs(1))]
    pallas_call x3, Pallas kernels: 13.2 us -> 9.2 us  [the longest x1 4.18 us: pair_bias(): pl.pallas_call(functools.partial(pair_kernel, batch), in_specs=[HBM] + [V...]
    ppermute x1, starting transfers between devices: 0.65 us -> 3.02 us  [body(): a0 = lax.ppermute(xa, AXES, long_pairs(0))]
    ppermute x3, starting transfers between devices: 6.55 us -> 4.35 us  [body(): others = [lax.ppermute(msg, 'col', shift_pairs(k)) for k in (1, 3, 2)]]
    unnamed x18 -> x17, local copies, waits for them, and re-layouts: 1.87 us -> 4 us
    ppermute x3, waiting for transfers between devices: 3.45 us -> 5.47 us  [body(): others = [lax.ppermute(msg, 'col', shift_pairs(k)) for k in (1, 3, 2)]]
    ppermute x1, starting transfers between devices: 0.01 us -> 0.81 us  [body(): p1 = lax.ppermute(pay1, ('sample', 'col'), side_pairs())]
  transfers between devices with their start and end apart: 12 -> 12, of which waited for: 6 -> 7; matrix products, arithmetic and copies ran while one was open for 5% -> 2% of each run, Pallas kernels for 19% -> 15%
where the time goes in v3:
time: 43.3 us; the launch traced here: 43 us
  starting transfers between devices  20.5 us (47%)
  Pallas kernels  10.3 us (24%)
  waiting for transfers between devices  8.05 us (19%)
  local copies, waits for them, and re-layouts  4.01 us (9%)
    ppermute x1, starting transfers between devices, body(): a1 = lax.ppermute(xa, AXES, long_pairs(1))  8.2 us
    ppermute x3, waiting for transfers between devices, body(): others = [lax.ppermute(msg, 'col', shift_pairs(k)) for k in (1, 3, 2)]  5.47 us
    ppermute x3, starting transfers between devices, body(): others = [lax.ppermute(msg, 'col', shift_pairs(k)) for k in (1, 3, 2)]  4.35 us
    pallas_call x1, Pallas kernels, pair_bias(): pl.pallas_call(functools.partial(pair_kernel, batch), in_specs=[HBM] + [V...  4.18 us
    unnamed x17, local copies, waits for them, and re-layouts  4 us
    ppermute x1, starting transfers between devices, body(): a0 = lax.ppermute(xa, AXES, long_pairs(0))  3.02 us
    pallas_call x1, Pallas kernels, attend(): pl.pallas_call(attend_kernel, in_specs=[VMEM] * 11, out_specs=[VMEM] * 3,...  2.71 us
    pallas_call x1, Pallas kernels, prepare(): pl.pallas_call(prepare_kernel, in_specs=[HBM] * 11, out_specs=[VMEM] * 9,...  2.32 us
  transfers between devices with their start and end apart: 12, of which 7 were waited for; matrix products, arithmetic and copies ran while one was open for 2% of the time, Pallas kernels for 15%

profile of v3, /device:TPU:8, one launch (start us, length us, event | category | flops | bytes accessed | tf_op | source)
XLA Modules:
  0.0 43.0 jit_solution(15640063081532216779)
XLA Ops:
  0.0 0.7 %constant_dynamic-update-slice_fusion.1 = bf16[128,96]{1,0:T(8,128)(2,1)S(1)} fusion(bf16[64,96]{1,0:T(8,128)(2,1)} %param.17), kind=kLoop, calls=%fused_computation.3 | loop fusion | bytes 28672
  0.7 0.7 %collective-permute-done = bf16[64,96]{1,0:T(8,128)(2,1)S(1)} collective-permute-done((bf16[64,96]{1,0:T(8,128)(2,1)}, bf16[64,96]{1,0:T(8,128)(2,1)S(1)}, u32[]{:S(2)}, u32[]{:S(2)}) %collective-permute-start) | collective-permute-done | bytes 12320 | tf_op jit(solution)/shard_map/ppermute | solution.py:412
  1.4 8.2 %collective-permute-start.2 = (bf16[128,96]{1,0:T(8,128)(2,1)S(1)}, bf16[128,96]{1,0:T(8,128)(2,1)S(1)}, u32[]{:S(2)}, u32[]{:S(2)}) collective-permute-start(bf16[128,96]{1,0:T(8,128)(2,1)S(1)} %constant_dynamic-update-slice_fusion), channel_id=1, source_target_pairs={{134,0},{150,1},{166,2},{182,3},{130,4},{146,5},{162,6},{178,7},{1... | collective-permute-start | bytes 73736 | tf_op jit(solution)/shard_map/ppermute | solution.py:415
  9.6 3.0 %collective-permute-start.1 = (bf16[128,96]{1,0:T(8,128)(2,1)S(1)}, bf16[128,96]{1,0:T(8,128)(2,1)S(1)}, u32[]{:S(2)}, u32[]{:S(2)}) collective-permute-start(bf16[128,96]{1,0:T(8,128)(2,1)S(1)} %constant_dynamic-update-slice_fusion), channel_id=1, source_target_pairs={{2,0},{18,1},{34,2},{50,3},{6,4},{22,5},{38,6},{54,7},{10,8},{26,9... | collective-permute-start | bytes 73736 | tf_op jit(solution)/shard_map/ppermute | solution.py:414
  12.6 2.3 %prepare.1 = (bf16[1248,128]{1,0:T(8,128)(2,1)}, bf16[672,128]{1,0:T(8,128)(2,1)}, bf16[4,96,384]{2,1,0:T(8,128)(2,1)}, bf16[96,128]{1,0:T(8,128)(2,1)}, bf16[12...) custom-call(bf16[96,384]{1,0:T(8,128)(2,1)} %bitcast.8, ...), custom_call_target="tpu_custom_call" | custom-call | tf_op jit(solution)/shard_map/prepare/pallas_call | solution.py:117
  15.0 0.5 %collective-permute-done.1 = bf16[128,96]{1,0:T(8,128)(2,1)S(1)} collective-permute-done((bf16[128,96]{1,0:T(8,128)(2,1)S(1)}, bf16[128,96]{1,0:T(8,128)(2,1)S(1)}, u32[]{:S(2)}, u32[]{:S(2)}) %collective-permute-start.1) | collective-permute-done | bytes 24608 | tf_op jit(solution)/shard_map/ppermute | solution.py:414
  15.4 0.8 %collective-permute-start.4 = (bf16[1248,128]{1,0:T(8,128)(2,1)}, bf16[1248,128]{1,0:T(8,128)(2,1)S(1)}, u32[]{:S(2)}, u32[]{:S(2)}) collective-permute-start(bf16[1248,128]{1,0:T(8,128)(2,1)} %get-tuple-element.35), channel_id=1, source_target_pairs={{0,1},{1,2},{2,3},{3,0},{64,67},{65,64},{66,65},{67,66},{128,129},... | collective-permute-start | bytes 958472 | tf_op jit(solution)/shard_map/ppermute | solution.py:424
  16.3 1.4 %collective-permute-start.5 = (bf16[672,128]{1,0:T(8,128)(2,1)}, bf16[672,128]{1,0:T(8,128)(2,1)S(1)}, u32[]{:S(2)}, u32[]{:S(2)}) collective-permute-start(bf16[672,128]{1,0:T(8,128)(2,1)} %get-tuple-element.36), channel_id=1, source_target_pairs={{0,2},{1,3},{2,0},{3,1},{4,6},{5,7},{6,4},{7,5},{8,10},{9,11},{10,... | collective-permute-start | bytes 516104 | tf_op jit(solution)/shard_map/ppermute | solution.py:425
  17.7 2.0 %collective-permute-start.3 = (bf16[320,96]{1,0:T(8,128)(2,1)S(1)}, bf16[320,96]{1,0:T(8,128)(2,1)S(1)}, u32[]{:S(2)}, u32[]{:S(2)}) collective-permute-start(bf16[320,96]{1,0:T(8,128)(2,1)S(1)} %pad_maximum_fusion.1), channel_id=1, source_target_pairs={{0,128},{64,192},{128,0},{192,64},{1,129},{65,193},{129,1},{193,65... | collective-permute-start | bytes 184328 | tf_op jit(solution)/shard_map/ppermute | solution.py:428
  19.7 0.9 %copy-done.1 = f32[128,256]{1,0:T(8,128)S(1)} copy-done((f32[128,256]{1,0:T(8,128)S(1)}, f32[128,256]{1,0:T(8,128)}, u32[]{:S(2)}) %copy-start.1) | copy-done | bytes 131096
  20.6 0.8 %copy-done.2 = s32[1,64,256]{2,1,0:T(8,128)S(1)} copy-done((s32[1,64,256]{2,1,0:T(8,128)S(1)}, s32[1,64,256]{2,1,0:T(8,128)}, u32[]{:S(2)}) %copy-start.2) | copy-done | bytes 65560
  21.4 0.8 %copy-done.3 = bf16[128,256]{1,0:T(8,128)(2,1)S(1)} copy-done((bf16[128,256]{1,0:T(8,128)(2,1)S(1)}, bf16[128,256]{1,0:T(8,128)(2,1)}, u32[]{:S(2)}) %copy-start.3) | copy-done | bytes 65560
  22.3 0.7 %copy-done.5 = bf16[16,128]{1,0:T(8,128)(2,1)S(1)} copy-done((bf16[16,128]{1,0:T(8,128)(2,1)S(1)}, bf16[16,128]{1,0:T(8,128)(2,1)}, u32[]{:S(2)}) %copy-start.5) | copy-done | bytes 4120
  22.9 4.2 %pair_bias.1.bias_all = bf16[64,16,256]{2,1,0:T(8,128)(2,1)S(1)} custom-call(bf16[64,256,128]{2,1,0:T(8,128)(2,1)} %pair.1, s32[64,256]{1,0:T(8,128)S(1)} %bitcast.7, bf16[128,256]{1,0:T(8,128)(2,1)S(1)} %copy-done.3, f32[128,256]{1,0:T(8,128)S(1)} %copy-done.1, bf16[16,128]{1,0:T(8,128)(2,1)S(1)} %copy-done.5), custom_call_target="tpu_custom_call" | custom-call | tf_op jit(solution)/shard_map/pair_bias/pallas_call | solution.py:182
  27.3 0.5 %collective-permute-start.8 = (bf16[672,128]{1,0:T(8,128)(2,1)S(1)}, bf16[672,128]{1,0:T(8,128)(2,1)S(1)}, u32[]{:S(2)}, u32[]{:S(2)}) collective-permute-start(bf16[672,128]{1,0:T(8,128)(2,1)S(1)} %collective-permute-done.5.p2), channel_id=1, source_target_pairs={{0,64},{64,0},{128,192},{192,128},{1,65},{65,1},{129,193},{193,129... | collective-permute-start | bytes 516104 | tf_op jit(solution)/shard_map/ppermute | solution.py:434
  27.8 0.2 collective-permute-start.6
  28.0 1.4 %collective-permute-done.6.sib = bf16[640,96]{1,0:T(8,128)(2,1)S(1)} collective-permute-done((bf16[640,96]{1,0:T(8,128)(2,1)S(1)}, bf16[640,96]{1,0:T(8,128)(2,1)S(1)}, u32[]{:S(2)}, u32[]{:S(2)}) %collective-permute-start.6) | collective-permute-done | bytes 122912 | tf_op jit(solution)/shard_map/ppermute | solution.py:432
  29.4 2.7 %attend.1 = (bf16[64,512]{1,0:T(8,128)(2,1)S(1)}, f32[64,384]{1,0:T(8,128)S(1)}, bf16[384,128]{1,0:T(8,128)(2,1)S(1)}) custom-call(bf16[640,96]{1,0:T(8,128)(2,1)S(1)} %pad_maximum_fusion.mn, bf16[640,96]{1,0:T(8,128)(2,1)S(1)} %collective-permute-done.6.sib, bf16[4,96,384]{2,1,0:T(8,128)(2,1)S(1)} %copy-done, bf16[96,128]{1,0:T(8,128)(2,1)S(1)} %copy-done.4, ...), custom_call_target="tpu_custom_call" | custom-call | tf_op jit(solution)/shard_map/attend/pallas_call | solution.py:322
  32.1 2.2 %collective-permute-start.11 = (bf16[64,512]{1,0:T(8,128)(2,1)S(1)}, bf16[64,512]{1,0:T(8,128)(2,1)S(1)}, u32[]{:S(2)}, u32[]{:S(2)}) collective-permute-start(bf16[64,512]{1,0:T(8,128)(2,1)S(1)} %get-tuple-element.48.m0), channel_id=1, source_target_pairs={{0,2},{1,3},{2,0},{3,1},{4,6},{5,7},{6,4},{7,5},{8,10},{9,11},{10,... | collective-permute-start | bytes 196616 | tf_op jit(solution)/shard_map/ppermute | solution.py:437
  34.3 2.1 %collective-permute-start.10 = (bf16[64,512]{1,0:T(8,128)(2,1)S(1)}, bf16[64,512]{1,0:T(8,128)(2,1)S(1)}, u32[]{:S(2)}, u32[]{:S(2)}) collective-permute-start(bf16[64,512]{1,0:T(8,128)(2,1)S(1)} %get-tuple-element.48.m0), channel_id=1, source_target_pairs={{0,3},{1,0},{2,1},{3,2},{4,7},{5,4},{6,5},{7,6},{8,11},{9,8},{10,9... | collective-permute-start | bytes 196616 | tf_op jit(solution)/shard_map/ppermute | solution.py:437
  36.5 1.5 %collective-permute-done.11.m3 = bf16[64,512]{1,0:T(8,128)(2,1)S(1)} collective-permute-done((bf16[64,512]{1,0:T(8,128)(2,1)S(1)}, bf16[64,512]{1,0:T(8,128)(2,1)S(1)}, u32[]{:S(2)}, u32[]{:S(2)}) %collective-permute-start.11) | collective-permute-done | bytes 65568 | tf_op jit(solution)/shard_map/ppermute | solution.py:437
  38.0 0.6 %collective-permute-done.10.m2 = bf16[64,512]{1,0:T(8,128)(2,1)S(1)} collective-permute-done((bf16[64,512]{1,0:T(8,128)(2,1)S(1)}, bf16[64,512]{1,0:T(8,128)(2,1)S(1)}, u32[]{:S(2)}, u32[]{:S(2)}) %collective-permute-start.10) | collective-permute-done | bytes 65568 | tf_op jit(solution)/shard_map/ppermute | solution.py:437
  38.6 3.3 %collective-permute-done.9.m1 = bf16[64,512]{1,0:T(8,128)(2,1)S(1)} collective-permute-done((bf16[64,512]{1,0:T(8,128)(2,1)S(1)}, bf16[64,512]{1,0:T(8,128)(2,1)S(1)}, u32[]{:S(2)}, u32[]{:S(2)}) %collective-permute-start.9) | collective-permute-done | bytes 65568 | tf_op jit(solution)/shard_map/ppermute | solution.py:437
  41.9 1.1 %combine.1 = bf16[64,96]{1,0:T(8,128)(2,1)} custom-call(bf16[64,512]{1,0:T(8,128)(2,1)S(1)} %get-tuple-element.48.m0, bf16[64,512]{1,0:T(8,128)(2,1)S(1)} %collective-permute-done.9.m1, bf16[64,512]{1,0:T(8,128)(2,1)S(1)} %collective-permute-done.10.m2, bf16[64,512]{1,0:T(8,128)(2,1)S(1)} %collective-permute-done.11.m3, ...), custom_call_target="tpu_custom_call" | custom-call | tf_op jit(solution)/shard_map/combine/pallas_call | solution.py:368
  (25 shorter events, 0.2 us)
Async XLA Ops:
  0.0 1.4 %collective-permute-start = (bf16[64,96]{1,0:T(8,128)(2,1)}, bf16[64,96]{1,0:T(8,128)(2,1)S(1)}, u32[]{:S(2)}, u32[]{:S(2)}) collective-permute-start(bf16[64,96]{1,0:T(8,128)(2,1)} %param.17), channel_id=1, source_target_pairs={{0,64},{64,0},{128,192},{192,128},{1,65},{65,1},{129,193},{193,129... | collective-permute-start | bytes 36872 | tf_op jit(solution)/shard_map/ppermute | solution.py:412
  1.4 13.6 %collective-permute-start.2 = (bf16[128,96]{1,0:T(8,128)(2,1)S(1)}, bf16[128,96]{1,0:T(8,128)(2,1)S(1)}, u32[]{:S(2)}, u32[]{:S(2)}) collective-permute-start(bf16[128,96]{1,0:T(8,128)(2,1)S(1)} %constant_dynamic-update-slice_fusion), channel_id=1, source_target_pairs={{134,0},{150,1},{166,2},{182,3},{130,4},{146,5},{162,6},{178,7},{1... | collective-permute-start | bytes 73736 | tf_op jit(solution)/shard_map/ppermute | solution.py:415
  9.6 5.8 %collective-permute-start.1 = (bf16[128,96]{1,0:T(8,128)(2,1)S(1)}, bf16[128,96]{1,0:T(8,128)(2,1)S(1)}, u32[]{:S(2)}, u32[]{:S(2)}) collective-permute-start(bf16[128,96]{1,0:T(8,128)(2,1)S(1)} %constant_dynamic-update-slice_fusion), channel_id=1, source_target_pairs={{2,0},{18,1},{34,2},{50,3},{6,4},{22,5},{38,6},{54,7},{10,8},{26,9... | collective-permute-start | bytes 73736 | tf_op jit(solution)/shard_map/ppermute | solution.py:414
  15.0 14.4 %copy-start = (bf16[4,96,384]{2,1,0:T(8,128)(2,1)S(1)}, bf16[4,96,384]{2,1,0:T(8,128)(2,1)}, u32[]{:S(2)}) copy-start(bf16[4,96,384]{2,1,0:T(8,128)(2,1)} %get-tuple-element.41.own_w) | copy-start | bytes 884740
  15.4 11.8 %collective-permute-start.4 = (bf16[1248,128]{1,0:T(8,128)(2,1)}, bf16[1248,128]{1,0:T(8,128)(2,1)S(1)}, u32[]{:S(2)}, u32[]{:S(2)}) collective-permute-start(bf16[1248,128]{1,0:T(8,128)(2,1)} %get-tuple-element.35), channel_id=1, source_target_pairs={{0,1},{1,2},{2,3},{3,0},{64,67},{65,64},{66,65},{67,66},{128,129},... | collective-permute-start | bytes 958472 | tf_op jit(solution)/shard_map/ppermute | solution.py:424
  16.3 10.9 %collective-permute-start.5 = (bf16[672,128]{1,0:T(8,128)(2,1)}, bf16[672,128]{1,0:T(8,128)(2,1)S(1)}, u32[]{:S(2)}, u32[]{:S(2)}) collective-permute-start(bf16[672,128]{1,0:T(8,128)(2,1)} %get-tuple-element.36), channel_id=1, source_target_pairs={{0,2},{1,3},{2,0},{3,1},{4,6},{5,7},{6,4},{7,5},{8,10},{9,11},{10,... | collective-permute-start | bytes 516104 | tf_op jit(solution)/shard_map/ppermute | solution.py:425
  17.7 9.4 %collective-permute-start.3 = (bf16[320,96]{1,0:T(8,128)(2,1)S(1)}, bf16[320,96]{1,0:T(8,128)(2,1)S(1)}, u32[]{:S(2)}, u32[]{:S(2)}) collective-permute-start(bf16[320,96]{1,0:T(8,128)(2,1)S(1)} %pad_maximum_fusion.1), channel_id=1, source_target_pairs={{0,128},{64,192},{128,0},{192,64},{1,129},{65,193},{129,1},{193,65... | collective-permute-start | bytes 184328 | tf_op jit(solution)/shard_map/ppermute | solution.py:428
  19.7 0.9 %copy-start.1 = (f32[128,256]{1,0:T(8,128)S(1)}, f32[128,256]{1,0:T(8,128)}, u32[]{:S(2)}) copy-start(f32[128,256]{1,0:T(8,128)} %get-tuple-element.38.gain_b) | copy-start | bytes 393220
  20.6 0.8 %copy-start.2 = (s32[1,64,256]{2,1,0:T(8,128)S(1)}, s32[1,64,256]{2,1,0:T(8,128)}, u32[]{:S(2)}) copy-start(s32[1,64,256]{2,1,0:T(8,128)} %param.15) | copy-start | bytes 196612
  21.4 0.8 %copy-start.3 = (bf16[128,256]{1,0:T(8,128)(2,1)S(1)}, bf16[128,256]{1,0:T(8,128)(2,1)}, u32[]{:S(2)}) copy-start(bf16[128,256]{1,0:T(8,128)(2,1)} %get-tuple-element.37.centre) | copy-start | bytes 196612
  22.3 0.7 %copy-start.5 = (bf16[16,128]{1,0:T(8,128)(2,1)S(1)}, bf16[16,128]{1,0:T(8,128)(2,1)}, u32[]{:S(2)}) copy-start(bf16[16,128]{1,0:T(8,128)(2,1)} %get-tuple-element.39.weight) | copy-start | bytes 12292
  22.9 6.4 %copy-start.4 = (bf16[96,128]{1,0:T(8,128)(2,1)S(1)}, bf16[96,128]{1,0:T(8,128)(2,1)}, u32[]{:S(2)}) copy-start(bf16[96,128]{1,0:T(8,128)(2,1)} %get-tuple-element.42.own_t) | copy-start | bytes 73732
  22.9 6.4 %copy-start.6 = (f32[1,384]{1,0:T(1,128)S(1)}, f32[1,384]{1,0:T(1,128)}, u32[]{:S(2)}) copy-start(f32[1,384]{1,0:T(1,128)} %get-tuple-element.45.gain) | copy-start | bytes 4612
  22.9 6.4 %copy-start.7 = (f32[1,256]{1,0:T(1,128)S(1)}, f32[1,256]{1,0:T(1,128)}, u32[]{:S(2)}) copy-start(f32[1,256]{1,0:T(1,128)} %get-tuple-element.46.term) | copy-start | bytes 3076
  27.2 2.1 %collective-permute-start.7 = (bf16[1248,128]{1,0:T(8,128)(2,1)S(1)}, bf16[1248,128]{1,0:T(8,128)(2,1)S(1)}, u32[]{:S(2)}, u32[]{:S(2)}) collective-permute-start(bf16[1248,128]{1,0:T(8,128)(2,1)S(1)} %collective-permute-done.4.p1), channel_id=1, source_target_pairs={{0,64},{64,0},{128,192},{192,128},{1,65},{65,1},{129,193},{193,129... | collective-permute-start | bytes 958472 | tf_op jit(solution)/shard_map/ppermute | solution.py:433
  27.3 2.1 %collective-permute-start.8 = (bf16[672,128]{1,0:T(8,128)(2,1)S(1)}, bf16[672,128]{1,0:T(8,128)(2,1)S(1)}, u32[]{:S(2)}, u32[]{:S(2)}) collective-permute-start(bf16[672,128]{1,0:T(8,128)(2,1)S(1)} %collective-permute-done.5.p2), channel_id=1, source_target_pairs={{0,64},{64,0},{128,192},{192,128},{1,65},{65,1},{129,193},{193,129... | collective-permute-start | bytes 516104 | tf_op jit(solution)/shard_map/ppermute | solution.py:434
  27.8 1.5 %collective-permute-start.6 = (bf16[640,96]{1,0:T(8,128)(2,1)S(1)}, bf16[640,96]{1,0:T(8,128)(2,1)S(1)}, u32[]{:S(2)}, u32[]{:S(2)}) collective-permute-start(bf16[640,96]{1,0:T(8,128)(2,1)S(1)} %pad_maximum_fusion.mn), channel_id=1, source_target_pairs={{0,64},{64,0},{128,192},{192,128},{1,65},{65,1},{129,193},{193,129... | collective-permute-start | bytes 368648 | tf_op jit(solution)/shard_map/ppermute | solution.py:432
  32.1 5.9 %collective-permute-start.11 = (bf16[64,512]{1,0:T(8,128)(2,1)S(1)}, bf16[64,512]{1,0:T(8,128)(2,1)S(1)}, u32[]{:S(2)}, u32[]{:S(2)}) collective-permute-start(bf16[64,512]{1,0:T(8,128)(2,1)S(1)} %get-tuple-element.48.m0), channel_id=1, source_target_pairs={{0,2},{1,3},{2,0},{3,1},{4,6},{5,7},{6,4},{7,5},{8,10},{9,11},{10,... | collective-permute-start | bytes 196616 | tf_op jit(solution)/shard_map/ppermute | solution.py:437
  34.3 4.3 %collective-permute-start.10 = (bf16[64,512]{1,0:T(8,128)(2,1)S(1)}, bf16[64,512]{1,0:T(8,128)(2,1)S(1)}, u32[]{:S(2)}, u32[]{:S(2)}) collective-permute-start(bf16[64,512]{1,0:T(8,128)(2,1)S(1)} %get-tuple-element.48.m0), channel_id=1, source_target_pairs={{0,3},{1,0},{2,1},{3,2},{4,7},{5,4},{6,5},{7,6},{8,11},{9,8},{10,9... | collective-permute-start | bytes 196616 | tf_op jit(solution)/shard_map/ppermute | solution.py:437
  36.4 5.5 %collective-permute-start.9 = (bf16[64,512]{1,0:T(8,128)(2,1)S(1)}, bf16[64,512]{1,0:T(8,128)(2,1)S(1)}, u32[]{:S(2)}, u32[]{:S(2)}) collective-permute-start(bf16[64,512]{1,0:T(8,128)(2,1)S(1)} %get-tuple-element.48.m0), channel_id=1, source_target_pairs={{0,1},{1,2},{2,3},{3,0},{4,5},{5,6},{6,7},{7,4},{8,9},{9,10},{10,1... | collective-permute-start | bytes 196616 | tf_op jit(solution)/shard_map/ppermute | solution.py:437
